TPU v7x, 256 devices: a whole 4x4x8 slice. The times are simulated.
256 devices in a mesh: lon: 64 (over x_hi, z, y), lat: 4 (over x_lo, core).
Axes of the slice: x: 4 (x_hi: 2, x_lo: 2; x = x_hi * 2 + x_lo), y: 4, z: 8, core: 2. Of those that a mesh axis runs over, the one named last changes fastest.
Arguments:
- tokens: bfloat16 [4, 24, 768, 1024], P(None, 'lat', 'lon'), may hold values from -6 to 6
- cotangent: bfloat16 [4, 24, 768, 1024], P(None, 'lat', 'lon'), may hold values from -16 to 16
- norm_scale_vector: bfloat16 [1024], replicated, may hold values from 0.099609375 to 1.8984375
- query_matrix: bfloat16 [1024, 1024], replicated, may hold values from -1 to 1
- key_matrix: bfloat16 [1024, 1024], replicated, may hold values from -1 to 1
- value_matrix: bfloat16 [1024, 1024], replicated, may hold values from -0.1875 to 0.1875
- output_matrix: bfloat16 [1024, 1024], replicated, may hold values from -0.1875 to 0.1875
- adapter_down_maps: bfloat16 [4, 1024, 32], replicated, may hold values from -0.1875 to 0.1875
- adapter_up_maps: bfloat16 [4, 32, 1024], replicated, may hold values from -1 to 1
Outputs:
- tokens_grad: bfloat16 [4, 24, 768, 1024], P(None, 'lat', 'lon')
- lora_down_grad: float32 [4096, 32], P(('lon', 'lat'))
- lora_up_grad: float32 [32, 4096], P(None, ('lon', 'lat'))
All inputs are finite; a program needn't handle non-finite values.
Results may differ from a plain program's by a relative error of at most 0.015.
The roundings to bfloat16 on the way count: a program that leaves them out, or rounds other values in their place, can miss the bound.
Values may be sent and summed in bfloat16 or wider, within the bound.
A program may use at most 128 MiB of HBM per device.

v0:
```python
import jax
import jax.numpy as jnp
from jax import lax
from jax.sharding import PartitionSpec as P

HEADS = 16
WLEV = 2
WLAT = 6
WLON = 12


EPS = 1e-05
NEG = -1e30


def from_behind(block, axis, distance):
    devices = range(lax.axis_size(axis))
    route = [((i - distance) % len(devices), i) for i in devices]
    return lax.ppermute(block, axis, route)


def normalize(values):
    center = values - jnp.mean(values, axis=-1, keepdims=True)
    spread = jnp.mean(center * center, axis=-1, keepdims=True)
    inverse = lax.rsqrt(spread + EPS)
    return (center * inverse, inverse)


def norm_back(upstream_gradient, norm_scale, centred, inverse):
    scaled = upstream_gradient.astype(jnp.float32) * norm_scale
    first_mean = jnp.mean(scaled, axis=-1, keepdims=True)
    second_mean = jnp.mean(scaled * centred, axis=-1, keepdims=True)
    return inverse * (scaled - first_mean - centred * second_mean)


def partition(region, span_lev, span_lat, span_lon):
    levels, lat_count, lon_count, features = region.shape
    tiles = region.reshape(
        levels // span_lev,
        span_lev,
        lat_count // span_lat,
        span_lat,
        lon_count // span_lon,
        span_lon,
        features,
    )
    tiles = tiles.transpose(0, 2, 4, 1, 3, 5, 6)
    return tiles.reshape(-1, span_lev * span_lat * span_lon, features)


def unpartition(windows, layout, span_lev, span_lat, span_lon):
    levels, lat_count, lon_count, features = layout
    tiles = windows.reshape(
        levels // span_lev,
        lat_count // span_lat,
        lon_count // span_lon,
        span_lev,
        span_lat,
        span_lon,
        features,
    )
    tiles = tiles.transpose(0, 3, 1, 4, 2, 5, 6)
    return tiles.reshape(levels, lat_count, lon_count, features)


def matrix_product(left, right):
    return jnp.dot(left, right, preferred_element_type=jnp.float32)


def level_forward(region):
    return jnp.concatenate([region[1:], region[:1]], 0)


def level_back(region):
    return jnp.concatenate([region[-1:], region[:-1]], 0)


def roll_in_four(arrays):
    half_lon = WLON // 2
    half_lat = WLAT // 2
    strips = from_behind(
        (
            arrays[0][:, :, :half_lon],
            arrays[1][:, :, :half_lon],
            arrays[2][:, :, :half_lon],
            arrays[3][:, :, :half_lon],
        ),
        "lon",
        -1,
    )
    arrays = [
        jnp.concatenate([arrays[projection_member][:, :, half_lon:], strips[projection_member]], 2)
        for projection_member in range(4)
    ]
    band_rows = from_behind(
        (
            arrays[0][:, :half_lat],
            arrays[1][:, :half_lat],
            arrays[2][:, :half_lat],
            arrays[3][:, :half_lat],
        ),
        "lat",
        -1,
    )
    arrays = [
        jnp.concatenate([arrays[projection_member][:, half_lat:], band_rows[projection_member]], 1)
        for projection_member in range(4)
    ]
    return [level_forward(tensor) for tensor in arrays]


def roll_out_four(arrays):
    half_lon = WLON // 2
    half_lat = WLAT // 2
    arrays = [level_back(tensor) for tensor in arrays]
    lat_count = arrays[0].shape[1]
    lon_count = arrays[0].shape[2]
    cut_lat = lat_count - half_lat
    cut_lon = lon_count - half_lon
    band_rows = from_behind(
        (
            arrays[0][:, cut_lat:],
            arrays[1][:, cut_lat:],
            arrays[2][:, cut_lat:],
            arrays[3][:, cut_lat:],
        ),
        "lat",
        1,
    )
    arrays = [
        jnp.concatenate([band_rows[projection_member], arrays[projection_member][:, :cut_lat]], 1)
        for projection_member in range(4)
    ]
    strips = from_behind(
        (
            arrays[0][:, :, cut_lon:],
            arrays[1][:, :, cut_lon:],
            arrays[2][:, :, cut_lon:],
            arrays[3][:, :, cut_lon:],
        ),
        "lon",
        1,
    )
    return [
        jnp.concatenate([strips[projection_member], arrays[projection_member][:, :, :cut_lon]], 2)
        for projection_member in range(4)
    ]


def forward_rows(
    normalized_rows, upstream_gradient, weight_list, adapter_down_maps, adapter_up_maps
):
    projected_rows = []
    lowrank_states = []
    for projection_member in range(3):
        lowrank_state = matrix_product(
            normalized_rows, adapter_down_maps[projection_member]
        ).astype(jnp.bfloat16)
        built_result = matrix_product(
            normalized_rows, weight_list[projection_member]
        ) + matrix_product(lowrank_state, adapter_up_maps[projection_member])
        projected_rows.append(built_result.astype(jnp.bfloat16))
        lowrank_states.append(lowrank_state)
    backward_output = matrix_product(upstream_gradient, adapter_up_maps[3].T).astype(jnp.bfloat16)
    attention_gradient = (
        matrix_product(upstream_gradient, weight_list[3].T)
        + matrix_product(backward_output, adapter_down_maps[3].T)
    ).astype(jnp.bfloat16)
    return (projected_rows, attention_gradient, lowrank_states, backward_output)


def attend(queries, key_rows, value_rows, attention_gradient, labels, heads):
    windows, window_extent, features = queries.shape
    head_size = features // heads

    def per_head(tensor):
        return tensor.reshape(windows, window_extent, heads, head_size)

    query_h = per_head(queries)
    key_h = per_head(key_rows)
    value_h = per_head(value_rows)
    grad_h = per_head(attention_gradient)
    factor = head_size ** (-0.5)
    scores = (
        jnp.einsum("wqhd,wkhd->whqk", query_h, key_h, preferred_element_type=jnp.float32) * factor
    )
    allowed = labels[:, None, :, None] == labels[:, None, None, :]
    scores = jnp.where(allowed, scores, NEG)
    raised = jnp.exp(scores - jnp.max(scores, axis=-1, keepdims=True))
    probs = raised / jnp.sum(raised, axis=-1, keepdims=True)
    probs_low = probs.astype(jnp.bfloat16)
    attended_rows = jnp.einsum(
        "whqk,wkhd->wqhd", probs_low, value_h, preferred_element_type=jnp.float32
    )
    dprob = jnp.einsum("wqhd,wkhd->whqk", grad_h, value_h, preferred_element_type=jnp.float32)
    dscore = (probs * (dprob - jnp.sum(dprob * probs, axis=-1, keepdims=True)) * factor).astype(
        jnp.bfloat16
    )
    dquery = jnp.einsum("whqk,wkhd->wqhd", dscore, key_h, preferred_element_type=jnp.float32)
    dkey = jnp.einsum("whqk,wqhd->wkhd", dscore, query_h, preferred_element_type=jnp.float32)
    dvalue = jnp.einsum("whqk,wqhd->wkhd", probs_low, grad_h, preferred_element_type=jnp.float32)

    def merged(tensor):
        return tensor.astype(jnp.bfloat16).reshape(windows, window_extent, features)

    return (merged(attended_rows), merged(dquery), merged(dkey), merged(dvalue))


def backward_rows(
    normalized_rows,
    upstream_gradient,
    attended_rows,
    gradient_list,
    lowrank_states,
    backward_output,
    weight_list,
    adapter_down_maps,
    adapter_up_maps,
):
    lowrank_output = matrix_product(attended_rows, adapter_down_maps[3]).astype(jnp.bfloat16)
    summed_rows = jnp.zeros(normalized_rows.shape, jnp.float32)
    gradient_couples = []
    for projection_member in range(3):
        gradient_value = gradient_list[projection_member]
        backward_lowrank = matrix_product(
            gradient_value, adapter_up_maps[projection_member].T
        ).astype(jnp.bfloat16)
        gradient_couples.append(
            (
                matrix_product(normalized_rows.T, backward_lowrank),
                matrix_product(lowrank_states[projection_member].T, gradient_value),
            )
        )
        summed_rows = (
            summed_rows
            + matrix_product(gradient_value, weight_list[projection_member].T)
            + matrix_product(backward_lowrank, adapter_down_maps[projection_member].T)
        )
    gradient_couples.append(
        (
            matrix_product(attended_rows.T, backward_output),
            matrix_product(lowrank_output.T, upstream_gradient),
        )
    )
    return (summed_rows.astype(jnp.bfloat16), gradient_couples)


def reduce_pair(down_part, up_part):
    return lax.psum((down_part, up_part), ("lon", "lat"))


def local(
    tokens,
    cotangent,
    norm_scale_vector,
    query_matrix,
    key_matrix,
    value_matrix,
    output_matrix,
    adapter_down_maps,
    adapter_up_maps,
):
    levels, lat_count, lon_count, features = tokens.shape
    layout = (levels, lat_count, lon_count, features)
    token_count = levels * lat_count * lon_count
    norm_scale = norm_scale_vector.astype(jnp.float32)
    centred, inverse = normalize(tokens.astype(jnp.float32))
    normed = (centred * norm_scale).astype(jnp.bfloat16)
    band_start = lax.axis_index("lat") * lat_count
    total_lats = lax.axis_size("lat") * lat_count
    level_flag = 2 * (jnp.arange(levels, dtype=jnp.int32) == levels - 1).astype(jnp.int32)
    band_flag = (
        band_start + jnp.arange(lat_count, dtype=jnp.int32) >= total_lats - WLAT // 2
    ).astype(jnp.int32)
    label_grid = (
        level_flag[:, None, None, None]
        + band_flag[None, :, None, None]
        + jnp.zeros((1, 1, lon_count, 1), jnp.int32)
    )
    labels = partition(label_grid, WLEV, WLAT, WLON)[:, :, 0]
    weight_list = (query_matrix, key_matrix, value_matrix, output_matrix)
    normalized_rows = normed.reshape(token_count, features)
    upstream_gradient = cotangent.reshape(token_count, features)
    projected_rows, attention_gradient, lowrank_states, backward_output = forward_rows(
        normalized_rows, upstream_gradient, weight_list, adapter_down_maps, adapter_up_maps
    )
    shifted = roll_in_four(
        [tensor.reshape(layout) for tensor in projected_rows + [attention_gradient]]
    )
    shaped = [partition(tensor, WLEV, WLAT, WLON) for tensor in shifted]
    attended_rows, dquery, dkey, dvalue = attend(
        shaped[0], shaped[1], shaped[2], shaped[3], labels, HEADS
    )
    returned = roll_out_four(
        [
            unpartition(tensor, layout, WLEV, WLAT, WLON)
            for tensor in (attended_rows, dquery, dkey, dvalue)
        ]
    )
    flattened_rows = [tensor.reshape(token_count, features) for tensor in returned]
    summed_rows, gradient_couples = backward_rows(
        normalized_rows,
        upstream_gradient,
        flattened_rows[0],
        flattened_rows[1:],
        lowrank_states,
        backward_output,
        weight_list,
        adapter_down_maps,
        adapter_up_maps,
    )
    dnormed = summed_rows.reshape(layout)
    tokens_grad = (
        cotangent.astype(jnp.float32) + norm_back(dnormed, norm_scale, centred, inverse)
    ).astype(jnp.bfloat16)
    devices = lax.axis_size("lon") * lax.axis_size("lat")
    grad_scale = float(token_count * devices) ** (-0.5)
    reduced = [reduce_pair(pair[0], pair[1]) for pair in gradient_couples]
    down_all = jnp.concatenate([pair[0] for pair in reduced], 0)
    up_all = jnp.concatenate([pair[1] for pair in reduced], 1)
    piece = down_all.shape[0] // devices
    start = lax.axis_index(("lon", "lat")) * piece
    down_own = lax.dynamic_slice_in_dim(down_all, start, piece, 0)
    up_own = lax.dynamic_slice_in_dim(up_all, start, piece, 1)
    return (tokens_grad, down_own * grad_scale, up_own * grad_scale)


def solution(mesh):
    placed = (
        P(None, "lat", "lon", None),
        P(None, "lat", "lon", None),
        P(),
        P(),
        P(),
        P(),
        P(),
        P(),
        P(),
    )
    return jax.shard_map(
        local,
        mesh=mesh,
        in_specs=placed,
        out_specs=(P(None, "lat", "lon", None), P(("lon", "lat"), None), P(None, ("lon", "lat"))),
        check_vma=False,
    )
```

profile of v0, /device:TPU:1, one launch (start us, length us, event | category | flops | bytes accessed | tf_op | source)
XLA Modules:
  0.0 560.0 jit_solution(15513115926197452646)
XLA Ops:
  22.5 11.3 %collective-permute-start.6 = (bf16[4,6,6,1024]{3,2,1,0:T(8,128)(2,1)}, bf16[4,6,6,1024]{3,2,1,0:T(8,128)(2,1)}, u32[]{:S(2)}, u32[]{:S(2)}) collective-permute-start(bf16[4,6,6,1024]{3,2,1,0:T(8,128)(2,1)} %get-tuple-element.26), channel_id=1, source_target_pairs={{4,0},{8,4},{12,8},{16,12},{20,16},{24,20},{28,24},{32,28},{36,32}... | collective-permute-start | bytes 884744 | tf_op jit(solution)/shard_map/ppermute | solution.py:19
  56.1 3.2 fusion.48
  81.4 2.8 copy.25
  90.0 2.9 copy.26
  98.7 2.8 copy.21
  101.5 5.6 fusion.138
  107.0 4.1 fusion.45
  111.2 2.8 copy.37
  114.0 2.8 reshape_transpose_reshape_reshape.15
  122.7 2.7 reshape_reshape_transpose_reshape.14
  125.5 14.0 %copy.24 = bf16[2,144,16,64]{1,3,2,0:T(8,128)(2,1)} copy(bf16[2,144,16,64]{3,2,1,0:T(8,128)(2,1)} %reshape_reshape_transpose_reshape.14) | data formatting | bytes 1179648 | tf_op jit(solution)/shard_map/reshape;reshape;transpose;reshape | solution.py:177
  139.5 4.6 fusion.139
  144.0 9.3 %fusion.41 = bf16[2,144,16,64]{1,3,2,0:T(8,128)(2,1)} fusion(bf16[2,144,16,64]{1,3,2,0:T(8,128)(2,1)} %copy.26, f32[2,16,144,144]{2,3,1,0:T(8,128)} %fusion.139, f32[2,16,144,144]{2,3,1,0:T(8,128)} %get-tuple-element.42, f32[2,16,144]{2,1,0:T(8,128)S(1)} %get-tuple-element.41), kind=kOutput, calls=%fused_computation.44 | convolution fusion | flops 89879184 | bytes 6506496 | tf_op jit(solution)/shard_map/whqk,wkhd->wqhd/dot_general | solution.py:199
  153.3 2.8 copy.28
  156.2 2.8 reshape_transpose_reshape_reshape.12
  162.6 9.4 %fusion.38 = bf16[2,144,16,64]{1,3,2,0:T(8,128)(2,1)} fusion(bf16[2,144,16,64]{1,3,2,0:T(8,128)(2,1)} %copy.21, f32[2,16,144,144]{2,3,1,0:T(8,128)} %fusion.139, f32[2,16,144,144]{2,3,1,0:T(8,128)} %get-tuple-element.42, f32[2,16,144]{2,1,0:T(8,128)S(1)} %get-tuple-element.41), kind=kOutput, calls=%fused_computation.43 | convolution fusion | flops 89879184 | bytes 6506496 | tf_op jit(solution)/shard_map/whqk,wqhd->wkhd/dot_general | solution.py:200
  172.0 4.7 fusion.44
  178.7 2.8 copy.31
  181.5 2.8 reshape_transpose_reshape_reshape.13
  187.9 2.8 copy.34
  190.7 2.8 reshape_transpose_reshape_reshape.14
  212.1 13.2 %collective-permute-done.9 = bf16[4,6,6,1024]{3,2,1,0:T(8,128)(2,1)S(1)} collective-permute-done((bf16[4,6,6,1024]{3,2,1,0:T(8,128)(2,1)S(1)}, bf16[4,6,6,1024]{3,2,1,0:T(8,128)(2,1)S(1)}, u32[]{:S(2)}, u32[]{:S(2)}) %collective-permute-start.9) | collective-permute-done | bytes 294944 | tf_op jit(solution)/shard_map/ppermute | solution.py:19
  266.2 3.5 fusion.37
  279.8 270.0 %all-reduce.3.cloned.1.call-done = (f32[1024,32]{0,1:T(8,128)}, f32[1024,32]{0,1:T(8,128)}, f32[1024,32]{0,1:T(8,128)}, f32[1024,32]{0,1:T(8,128)}, f32[32,1024]...) async-done(((f32[1024,32]{0,1:T(8,128)}, f32[1024,32]{0,1:T(8,128)}, f32[1024,32]{0,1:T(8,128)}, f32[1024,32]{0,1:T(8,128)}, ...) | async-done | bytes 1048592 | tf_op jit(solution)/shard_map/psum | solution.py:249
  (218 shorter events, 158.3 us)
Async XLA Ops:
  7.2 9.2 %copy-start = (bf16[1024,1024]{1,0:T(8,128)(2,1)S(1)}, bf16[1024,1024]{1,0:T(8,128)(2,1)}, u32[]{:S(2)}) copy-start(bf16[1024,1024]{1,0:T(8,128)(2,1)} %param.14) | copy-start | bytes 6291460
  7.2 542.6 %all-reduce.3.cloned.1.call-start = ((), (), s32[]{:S(2)}) async-start(), calls=%async_computation | async-start | bytes 2097152 | tf_op jit(solution)/shard_map/psum | solution.py:249
  20.0 15.8 %copy-start.39 = (bf16[1024,1024]{1,0:T(8,128)(2,1)S(1)}, bf16[1024,1024]{1,0:T(8,128)(2,1)}, u32[]{:S(2)}) copy-start(bf16[1024,1024]{1,0:T(8,128)(2,1)} %param.13) | copy-start | bytes 6291460
  22.5 41.7 %collective-permute-start.6 = (bf16[4,6,6,1024]{3,2,1,0:T(8,128)(2,1)}, bf16[4,6,6,1024]{3,2,1,0:T(8,128)(2,1)}, u32[]{:S(2)}, u32[]{:S(2)}) collective-permute-start(bf16[4,6,6,1024]{3,2,1,0:T(8,128)(2,1)} %get-tuple-element.26), channel_id=1, source_target_pairs={{4,0},{8,4},{12,8},{16,12},{20,16},{24,20},{28,24},{32,28},{36,32}... | collective-permute-start | bytes 884744 | tf_op jit(solution)/shard_map/ppermute | solution.py:19
  41.9 25.7 %collective-permute-start = (bf16[4,6,6,1024]{3,2,1,0:T(8,128)(2,1)}, bf16[4,6,6,1024]{3,2,1,0:T(8,128)(2,1)}, u32[]{:S(2)}, u32[]{:S(2)}) collective-permute-start(bf16[4,6,6,1024]{3,2,1,0:T(8,128)(2,1)} %get-tuple-element.32), channel_id=1, source_target_pairs={{4,0},{8,4},{12,8},{16,12},{20,16},{24,20},{28,24},{32,28},{36,32}... | collective-permute-start | bytes 884744 | tf_op jit(solution)/shard_map/ppermute | solution.py:19
  50.4 19.7 %collective-permute-start.2 = (bf16[4,6,6,1024]{3,2,1,0:T(8,128)(2,1)}, bf16[4,6,6,1024]{3,2,1,0:T(8,128)(2,1)}, u32[]{:S(2)}, u32[]{:S(2)}) collective-permute-start(bf16[4,6,6,1024]{3,2,1,0:T(8,128)(2,1)} %get-tuple-element.36), channel_id=1, source_target_pairs={{4,0},{8,4},{12,8},{16,12},{20,16},{24,20},{28,24},{32,28},{36,32}... | collective-permute-start | bytes 884744 | tf_op jit(solution)/shard_map/ppermute | solution.py:19
  63.6 9.4 %collective-permute-start.4 = (bf16[4,6,6,1024]{3,2,1,0:T(8,128)(2,1)}, bf16[4,6,6,1024]{3,2,1,0:T(8,128)(2,1)}, u32[]{:S(2)}, u32[]{:S(2)}) collective-permute-start(bf16[4,6,6,1024]{3,2,1,0:T(8,128)(2,1)} %get-tuple-element.40), channel_id=1, source_target_pairs={{4,0},{8,4},{12,8},{16,12},{20,16},{24,20},{28,24},{32,28},{36,32}... | collective-permute-start | bytes 884744 | tf_op jit(solution)/shard_map/ppermute | solution.py:19
  64.2 5.9 %copy-start.21 = (bf16[4,6,6,1024]{3,2,1,0:T(8,128)(2,1)S(1)}, bf16[4,6,6,1024]{3,2,1,0:T(8,128)(2,1)}, u32[]{:S(2)}) copy-start(bf16[4,6,6,1024]{3,2,1,0:T(8,128)(2,1)} %get-tuple-element.35) | copy-start | bytes 884740
  65.7 11.9 %collective-permute-start.7 = (bf16[4,3,12,1024]{3,2,1,0:T(8,128)(2,1)S(1)}, bf16[4,3,12,1024]{3,2,1,0:T(8,128)(2,1)S(1)}, u32[]{:S(2)}, u32[]{:S(2)}) collective-permute-start(bf16[4,3,12,1024]{3,2,1,0:T(8,128)(2,1)S(1)} %get-tuple-element.24), channel_id=1, source_target_pairs={{1,0},{2,1},{3,2},{0,3},{5,4},{6,5},{7,6},{4,7},{9,8},{10,9},{11,1... | collective-permute-start | bytes 884744 | tf_op jit(solution)/shard_map/ppermute | solution.py:19
  69.8 14.4 %collective-permute-start.1 = (bf16[4,3,12,1024]{3,2,1,0:T(8,128)(2,1)}, bf16[4,3,12,1024]{3,2,1,0:T(8,128)(2,1)}, u32[]{:S(2)}, u32[]{:S(2)}) collective-permute-start(bf16[4,3,12,1024]{3,2,1,0:T(8,128)(2,1)} %get-tuple-element.30), channel_id=1, source_target_pairs={{1,0},{2,1},{3,2},{0,3},{5,4},{6,5},{7,6},{4,7},{9,8},{10,9},{11,1... | collective-permute-start | bytes 884744 | tf_op jit(solution)/shard_map/ppermute | solution.py:19
  72.3 20.6 %collective-permute-start.3 = (bf16[4,3,12,1024]{3,2,1,0:T(8,128)(2,1)}, bf16[4,3,12,1024]{3,2,1,0:T(8,128)(2,1)}, u32[]{:S(2)}, u32[]{:S(2)}) collective-permute-start(bf16[4,3,12,1024]{3,2,1,0:T(8,128)(2,1)} %get-tuple-element.34), channel_id=1, source_target_pairs={{1,0},{2,1},{3,2},{0,3},{5,4},{6,5},{7,6},{4,7},{9,8},{10,9},{11,1... | collective-permute-start | bytes 884744 | tf_op jit(solution)/shard_map/ppermute | solution.py:19
  75.2 44.6 %collective-permute-start.5 = (bf16[4,3,12,1024]{3,2,1,0:T(8,128)(2,1)}, bf16[4,3,12,1024]{3,2,1,0:T(8,128)(2,1)}, u32[]{:S(2)}, u32[]{:S(2)}) collective-permute-start(bf16[4,3,12,1024]{3,2,1,0:T(8,128)(2,1)} %get-tuple-element.38), channel_id=1, source_target_pairs={{1,0},{2,1},{3,2},{0,3},{5,4},{6,5},{7,6},{4,7},{9,8},{10,9},{11,1... | collective-permute-start | bytes 884744 | tf_op jit(solution)/shard_map/ppermute | solution.py:19
  172.0 5.7 %copy-start.17 = (bf16[1,6,12,1024]{3,2,1,0:T(8,128)(2,1)S(1)}, bf16[1,6,12,1024]{3,2,1,0:T(8,128)(2,1)}, u32[]{:S(2)}) copy-start(bf16[1,6,12,1024]{3,2,1,0:T(8,128)(2,1)} %slice.255) | copy-start | bytes 442372
  177.5 20.5 %collective-permute-start.14 = (bf16[4,3,12,1024]{3,2,1,0:T(8,128)(2,1)}, bf16[4,3,12,1024]{3,2,1,0:T(8,128)(2,1)}, u32[]{:S(2)}, u32[]{:S(2)}) collective-permute-start(bf16[4,3,12,1024]{3,2,1,0:T(8,128)(2,1)} %fusion.67), channel_id=1, source_target_pairs={{3,0},{0,1},{1,2},{2,3},{7,4},{4,5},{5,6},{6,7},{11,8},{8,9},{9,10... | collective-permute-start | bytes 884744 | tf_op jit(solution)/shard_map/ppermute | solution.py:19
  195.7 5.7 %collective-permute-start.8 = (bf16[4,3,12,1024]{3,2,1,0:T(8,128)(2,1)}, bf16[4,3,12,1024]{3,2,1,0:T(8,128)(2,1)S(1)}, u32[]{:S(2)}, u32[]{:S(2)}) collective-permute-start(bf16[4,3,12,1024]{3,2,1,0:T(8,128)(2,1)} %fusion.70), channel_id=1, source_target_pairs={{3,0},{0,1},{1,2},{2,3},{7,4},{4,5},{5,6},{6,7},{11,8},{8,9},{9,10... | collective-permute-start | bytes 884744 | tf_op jit(solution)/shard_map/ppermute | solution.py:19
  196.2 9.1 %collective-permute-start.10 = (bf16[4,3,12,1024]{3,2,1,0:T(8,128)(2,1)S(1)}, bf16[4,3,12,1024]{3,2,1,0:T(8,128)(2,1)S(1)}, u32[]{:S(2)}, u32[]{:S(2)}) collective-permute-start(bf16[4,3,12,1024]{3,2,1,0:T(8,128)(2,1)S(1)} %fusion.69), channel_id=1, source_target_pairs={{3,0},{0,1},{1,2},{2,3},{7,4},{4,5},{5,6},{6,7},{11,8},{8,9},{9,10... | collective-permute-start | bytes 884744 | tf_op jit(solution)/shard_map/ppermute | solution.py:19
  197.4 12.1 %collective-permute-start.12 = (bf16[4,3,12,1024]{3,2,1,0:T(8,128)(2,1)S(1)}, bf16[4,3,12,1024]{3,2,1,0:T(8,128)(2,1)S(1)}, u32[]{:S(2)}, u32[]{:S(2)}) collective-permute-start(bf16[4,3,12,1024]{3,2,1,0:T(8,128)(2,1)S(1)} %fusion.68), channel_id=1, source_target_pairs={{3,0},{0,1},{1,2},{2,3},{7,4},{4,5},{5,6},{6,7},{11,8},{8,9},{9,10... | collective-permute-start | bytes 884744 | tf_op jit(solution)/shard_map/ppermute | solution.py:19
  200.1 32.3 %collective-permute-start.15 = (bf16[4,6,6,1024]{3,2,1,0:T(8,128)(2,1)}, bf16[4,6,6,1024]{3,2,1,0:T(8,128)(2,1)}, u32[]{:S(2)}, u32[]{:S(2)}) collective-permute-start(bf16[4,6,6,1024]{3,2,1,0:T(8,128)(2,1)} %get-tuple-element.17), channel_id=1, source_target_pairs={{252,0},{0,4},{4,8},{8,12},{12,16},{16,20},{20,24},{24,28},{28,32}... | collective-permute-start | bytes 884744 | tf_op jit(solution)/shard_map/ppermute | solution.py:19
  201.7 23.6 %collective-permute-start.9 = (bf16[4,6,6,1024]{3,2,1,0:T(8,128)(2,1)S(1)}, bf16[4,6,6,1024]{3,2,1,0:T(8,128)(2,1)S(1)}, u32[]{:S(2)}, u32[]{:S(2)}) collective-permute-start(bf16[4,6,6,1024]{3,2,1,0:T(8,128)(2,1)S(1)} %get-tuple-element.19), channel_id=1, source_target_pairs={{252,0},{0,4},{4,8},{8,12},{12,16},{16,20},{20,24},{24,28},{28,32}... | collective-permute-start | bytes 884744 | tf_op jit(solution)/shard_map/ppermute | solution.py:19
  206.4 32.1 %collective-permute-start.11 = (bf16[4,6,6,1024]{3,2,1,0:T(8,128)(2,1)}, bf16[4,6,6,1024]{3,2,1,0:T(8,128)(2,1)}, u32[]{:S(2)}, u32[]{:S(2)}) collective-permute-start(bf16[4,6,6,1024]{3,2,1,0:T(8,128)(2,1)} %get-tuple-element.21), channel_id=1, source_target_pairs={{252,0},{0,4},{4,8},{8,12},{12,16},{16,20},{20,24},{24,28},{28,32}... | collective-permute-start | bytes 884744 | tf_op jit(solution)/shard_map/ppermute | solution.py:19
  210.6 38.7 %collective-permute-start.13 = (bf16[4,6,6,1024]{3,2,1,0:T(8,128)(2,1)}, bf16[4,6,6,1024]{3,2,1,0:T(8,128)(2,1)}, u32[]{:S(2)}, u32[]{:S(2)}) collective-permute-start(bf16[4,6,6,1024]{3,2,1,0:T(8,128)(2,1)} %get-tuple-element.27), channel_id=1, source_target_pairs={{252,0},{0,4},{4,8},{8,12},{12,16},{16,20},{20,24},{24,28},{28,32}... | collective-permute-start | bytes 884744 | tf_op jit(solution)/shard_map/ppermute | solution.py:19
  240.8 6.0 %copy-start.25 = (bf16[4,1024,32]{1,2,0:T(8,128)(2,1)S(1)}, bf16[4,1024,32]{1,2,0:T(8,128)(2,1)}, u32[]{:S(2)}) copy-start(bf16[4,1024,32]{1,2,0:T(8,128)(2,1)} %param.16) | copy-start | bytes 786436
  253.6 6.4 %copy-start.35 = (bf16[288,32]{0,1:T(8,128)(2,1)S(1)}, bf16[288,32]{0,1:T(8,128)(2,1)}, u32[]{:S(2)}) copy-start(bf16[288,32]{0,1:T(8,128)(2,1)} %convolution_convert_fusion.4) | copy-start | bytes 55300
  257.0 7.2 %copy-start.36 = (bf16[288,32]{0,1:T(8,128)(2,1)}, bf16[288,32]{0,1:T(8,128)(2,1)S(1)}, u32[]{:S(2)}) copy-start(bf16[288,32]{0,1:T(8,128)(2,1)S(1)} %convolution_convert_fusion.3) | copy-start | bytes 55300
  (34 other events, 98.9 us)
Sparse Core Ops, SparseCore 0:
  276.5 273.2 all-reduce.2
where the time goes:
time: 571 us; the launch traced here: 560 us
  waiting for transfers between devices  287 us (50%)
  local copies, waits for them, and re-layouts  110 us (19%)
  matrix products  82 us (14%)
  other arithmetic  40.3 us (7%)
  starting transfers between devices  24.9 us (4%)
  between operations  14.9 us (3%)
    psum x1, waiting for transfers between devices, reduce_pair(): return lax.psum((down_part, up_part), ('lon', 'lat'))  270 us
    dot_general x29, matrix products, matrix_product(): return jnp.dot(left, right, preferred_element_type=jnp.float32)  44.3 us
    another operation x8, local copies, waits for them, and re-layouts, per_head(): return tensor.reshape(windows, window_extent, heads, head_size)  33.4 us
    ppermute x16, starting transfers between devices, from_behind(): return lax.ppermute(block, axis, route)  24.9 us
    ppermute x16, waiting for transfers between devices, from_behind(): return lax.ppermute(block, axis, route)  17.4 us
    slice x8, local copies, waits for them, and re-layouts, level_back(): return jnp.concatenate([region[-1:], region[:-1]], 0)  12.2 us
  transfers between devices with their start and end apart: 17, of which 4 were waited for; matrix products, arithmetic and copies ran while one was open for 23% of the time, Pallas kernels for 0%

commit v1 on v0

v1 whole, which is shorter than its diff:
```python
import functools

import jax
import jax.numpy as jnp
import numpy as np
from jax import lax
from jax.experimental import pallas as pl
from jax.experimental.pallas import tpu as pltpu
from jax.sharding import PartitionSpec as P

MESH = pl.DeviceIdType.MESH
BF = jnp.bfloat16
F32 = jnp.float32
EPS = 1e-05
NEG = -1e30
D = 1024
WIN = 144
TOK = 2 * WIN
LEVELS = ((1, 2), (3, 0))
OWN = (3, 0)
VMEM_LIMIT = 60 * 1024 * 1024


def permutation_table():
    table = np.zeros((592, 128), np.float32)

    def source(h, t):
        return (t // 18) * 48 + (t // 6 % 3) * 16 + 6 * h + t % 6

    for h in range(2):
        for t in range(32):
            table[32 * h + t, source(h, t)] = 1
            table[192 + source(h, t), 32 * h + t] = 1
        for k in range(4):
            for t in range(4):
                table[64 + 32 * k + 16 * h + 4 * k + t, source(h, 32 + t)] = 1
                table[288 + 96 * 0 + source(h, 32 + t), 32 * k + 16 * h + 4 * k + t] = 1
    for p in range(4):
        for k in range(4):
            for t in range(4):
                table[384 + 16 * k + 4 * p + t, 16 * p + 4 * k + t] = 1
                table[448 + 16 * p + 4 * k + t, 16 * k + 4 * p + t] = 1
    return table[:512]


def dot(a, b):
    return jnp.dot(a, b, preferred_element_type=F32)


def dot_nt(a, b):
    return lax.dot_general(a, b, (((1,), (1,)), ((), ())), preferred_element_type=F32)


def dot_tn(a, b):
    return lax.dot_general(a, b, (((0,), (0,)), ((), ())), preferred_element_type=F32)


def neighbour(sizes, lat_step, lon_step):
    lon = lax.rem(lax.axis_index("lon") + lon_step + sizes["lon"], sizes["lon"])
    lat = lax.rem(lax.axis_index("lat") + lat_step + sizes["lat"], sizes["lat"])
    return (lon, lat)


def steps_of(w, p):
    differs = p ^ OWN[w]
    sign = -1 if w == 0 else 1
    return sign * (differs >> 1), sign * (differs & 1)


def moving_pieces():
    return [(w, p) for w in range(2) for p in range(4) if p != OWN[w]]


def ring_of(sizes):
    return [neighbour(sizes, *steps_of(w, p)) for w, p in moving_pieces()]


def stage_slabs(array_ref, stage):
    stage[...] = jnp.zeros_like(stage)
    for w in range(2):
        for lv in range(2):
            for a in range(6):
                row = lv * 48 + (a % 3) * 16
                stage[w, a // 3, row : row + 12, :] = array_ref[LEVELS[w][lv], a]


def pack(stage, table, main, tail):
    for w in range(2):
        for ah in range(2):
            rows = stage[w, ah]
            packed = dot(table[0:64, 0:96], rows).astype(BF)
            main[w, 2 * ah] = packed[0:32]
            main[w, 2 * ah + 1] = packed[32:64]
            ends = jnp.zeros((32, 256), F32)
            for k in range(4):
                ends = ends + dot(
                    table[64 + 32 * k : 96 + 32 * k, 0:96], rows[:, 256 * k : 256 * k + 256]
                )
            ends = ends.astype(BF)
            tail[w, 2 * ah] = ends[0:16]
            tail[w, 2 * ah + 1] = ends[16:32]


def tails_to_window(table, tails, window, first):
    stacked = tails.reshape(64, 256)
    for k in range(4):
        window[first + 128 : first + 144, 256 * k : 256 * k + 256] = dot(
            table[384 + 16 * k : 400 + 16 * k, 0:64], stacked
        ).astype(BF)


def window_to_tails(table, rows):
    ends = jnp.zeros((64, 256), F32)
    for k in range(4):
        ends = ends + dot(
            table[448:512, 16 * k : 16 * k + 16], rows[:, 256 * k : 256 * k + 256]
        )
    return ends.astype(BF).reshape(4, 16, 256)


def unpack(table, main, tail, out_ref):
    for w in range(2):
        for ah in range(2):
            ends = jnp.concatenate([tail[w, 2 * ah], tail[w, 2 * ah + 1]], 0)
            rows = jnp.concatenate([main[w, 2 * ah], main[w, 2 * ah + 1]], 0)
            for k in range(4):
                cols = slice(256 * k, 256 * k + 256)
                slabs = (
                    dot(table[192:288, 0:64], rows[:, cols])
                    + dot(table[288:384, 32 * k : 32 * k + 32], ends)
                ).astype(BF)
                for lv in range(2):
                    for a in range(3):
                        row = lv * 48 + a * 16
                        out_ref[LEVELS[w][lv], 3 * ah + a, :, cols] = slabs[row : row + 12]


def barrier_with(devices):
    barrier = pltpu.get_barrier_semaphore()
    for device in devices:
        pl.semaphore_signal(barrier, inc=1, device_id=device, device_id_type=MESH)
    pl.semaphore_wait(barrier, len(devices))


def remote(src, dst, send, recv, device):
    return pltpu.make_async_remote_copy(
        src_ref=src, dst_ref=dst, send_sem=send, recv_sem=recv, device_id=device, device_id_type=MESH
    )


def in_copies(sizes, which, main, tail, window, tails, send, recv):
    copies = []
    for w, p in moving_pieces():
        device = neighbour(sizes, *steps_of(w, p))
        copies.append(
            remote(
                main.at[w, p],
                window.at[pl.ds(WIN * w + 32 * p, 32)],
                send.at[which, w, p, 0],
                recv.at[which, w, p, 0],
                device,
            )
        )
        copies.append(
            remote(
                tail.at[w, p],
                tails.at[w, p],
                send.at[which, w, p, 1],
                recv.at[which, w, p, 1],
                device,
            )
        )
    return copies


def keep_own(main, tail, window, tails):
    for w in range(2):
        p = OWN[w]
        window[WIN * w + 32 * p : WIN * w + 32 * p + 32, :] = main[w, p]
        tails[w, p] = tail[w, p]


def exchange_in(sizes, tok, cot, table, w_tok, w_cot, stage, main, tail, tails, send, recv):
    barrier_with(ring_of(sizes))
    copies = []
    for which, (array, window) in enumerate(((tok, w_tok), (cot, w_cot))):
        stage_slabs(array, stage)
        pack(stage, table, main.at[which], tail.at[which])
        own = in_copies(
            sizes, which, main.at[which], tail.at[which], window, tails.at[which], send, recv
        )
        for copy in own:
            copy.start()
        copies.append(own)
        keep_own(main.at[which], tail.at[which], window, tails.at[which])
    for which, window in enumerate((w_tok, w_cot)):
        for copy in copies[which]:
            copy.wait()
        for w in range(2):
            tails_to_window(table, tails[which, w], window, WIN * w)


def slot_lanes(values, slots):
    lane = lax.broadcasted_iota(jnp.int32, values.shape, 1) // 32
    keep = lane == slots[0]
    for slot in slots[1:]:
        keep = keep | (lane == slot)
    return jnp.where(keep, values, 0.0)


def norm_rows(w_tok, scale, hs, mean, rstd):
    gain = scale[...].astype(F32)

    def body(i, carry):
        rows = pl.ds(pl.multiple_of(i * 32, 32), 32)
        x = w_tok[rows, :].astype(F32)
        mu = jnp.mean(x, axis=-1, keepdims=True)
        center = x - mu
        inverse = lax.rsqrt(jnp.mean(center * center, axis=-1, keepdims=True) + EPS)
        mean[rows, :] = mu
        rstd[rows, :] = inverse
        hs[rows, :] = (center * inverse * gain).astype(BF)
        return carry

    lax.fori_loop(0, TOK // 32, body, 0)


def adapter_tables(down, acat):
    acat[...] = jnp.concatenate([down[n] for n in range(4)], 1)


def project(hs, w_cot, weights, up, acat, low, back, q, k, v, da):
    ups = up[...].reshape(128, D)
    low[...] = dot(hs[...], acat[...]).astype(BF)
    back[...] = slot_lanes(dot_nt(w_cot[...], ups), (3,)).astype(BF)
    lows = [slot_lanes(low[...].astype(F32), (n,)).astype(BF) for n in range(3)]
    wq, wk, wv, wo = weights
    for c in range(4):
        cols = slice(256 * c, 256 * c + 256)
        for n, (w, out) in enumerate(((wq, q), (wk, k), (wv, v))):
            out[:, cols] = (dot(hs[...], w[:, cols]) + dot(lows[n], ups[:, cols])).astype(BF)
        da[:, cols] = (dot_nt(w_cot[...], wo[cols, :]) + dot_nt(back[...], acat[cols, :])).astype(BF)


def make_bias(sizes, bias):
    lat = lax.axis_index("lat")

    def coordinates(r):
        tail = r >= 128
        piece = jnp.where(tail, (r - 128) // 4, r // 32)
        t = jnp.where(tail, 32 + r % 4, r % 32)
        return (piece < 2).astype(jnp.int32), (t >= 18).astype(jnp.int32)

    key_ah, key_lv = coordinates(lax.broadcasted_iota(jnp.int32, (WIN, 4 * WIN), 0))
    c = lax.broadcasted_iota(jnp.int32, (WIN, 4 * WIN), 1)
    for n in (3, 2, 1):
        c = jnp.where(c >= n * WIN, c - n * WIN, c)
    query_ah, query_lv = coordinates(c)
    for w in range(2):
        last = (lat == (sizes["lat"] - 1 if w == 0 else 0)).astype(jnp.int32)
        differs = (key_ah != query_ah).astype(jnp.int32) * last
        if w == 1:
            differs = differs + (key_lv != query_lv).astype(jnp.int32)
        bias[w] = jnp.where(differs > 0, NEG, 0.0).astype(F32)


def attend(q, k, v, da, bias, at, dq, dk, dv):
    lane = lax.broadcasted_iota(jnp.int32, (1, 256), 1) // 64
    masks = [(lane == h).astype(F32).astype(BF) for h in range(4)]
    lanes = lax.broadcasted_iota(jnp.int32, (WIN, 256), 1) // 64

    def stacked(values):
        return jnp.concatenate([values * mask for mask in masks], 0)

    def own_blocks(values):
        result = values[0:WIN]
        for h in range(1, 4):
            result = jnp.where(lanes == h, values[WIN * h : WIN * h + WIN], result)
        return result

    def body(c, carry):
        cols = pl.ds(pl.multiple_of(c * 256, 256), 256)
        for w in range(2):
            rows = pl.ds(WIN * w, WIN)
            kk = k[rows, cols]
            vv = v[rows, cols]
            q4 = stacked(q[rows, cols] * jnp.asarray(0.125, BF))
            d4 = stacked(da[rows, cols])
            s = dot_nt(kk, q4) + bias[w]
            e = jnp.exp(s - jnp.max(s, axis=0, keepdims=True))
            p = e * (1.0 / jnp.sum(e, axis=0, keepdims=True))
            dp = dot_nt(vv, d4)
            ds = (p * (dp - jnp.sum(dp * p, axis=0, keepdims=True))).astype(BF)
            pb = p.astype(BF)
            dv[rows, cols] = dot(pb, d4).astype(BF)
            dk[rows, cols] = dot(ds, q4).astype(BF)
            at[rows, cols] = own_blocks(dot_tn(pb, vv)).astype(BF)
            dq[rows, cols] = (own_blocks(dot_tn(ds, kk)) * 0.125).astype(BF)
        return carry

    lax.fori_loop(0, 4, body, 0)


def lora_partials(hs, w_cot, at, dq, dk, dv, up, acat, low, back, gt):
    ups = up[...].reshape(128, D)
    lane = lax.broadcasted_iota(jnp.int32, (TOK, 128), 1) // 32
    backs = back[...].astype(F32)
    for n, d in enumerate((dq, dk, dv)):
        backs = jnp.where(lane == n, dot_nt(d[...], ups), backs)
    back[...] = backs.astype(BF)
    lows = jnp.where(lane == 3, dot(at[...], acat[...]), low[...].astype(F32))
    back_t = backs.T.astype(BF)
    low_t = lows.T.astype(BF)
    for c in range(4):
        cols = slice(256 * c, 256 * c + 256)
        own_down = dot(back_t[0:96], hs[:, cols])
        last_down = dot(back_t[96:128], at[:, cols])
        ups_own = [dot(low_t[32 * n : 32 * n + 32], d[:, cols]) for n, d in enumerate((dq, dk, dv, w_cot))]
        parts = []
        for n in range(4):
            parts.append(own_down[32 * n : 32 * n + 32] if n < 3 else last_down)
            parts.append(ups_own[n])
        block = jnp.concatenate(parts, 0)
        for half in range(2):
            turned = block[:, 128 * half : 128 * half + 128].T.astype(BF)
            for b in range(8):
                f = 16 * c + 8 * half + b
                gt[f % 2, f // 2 % 2, f // 4 % 4, f // 16] = turned[16 * b : 16 * b + 16]


def input_gradient(w_tok, w_cot, scale, weights, dq, dk, dv, acat, back, mean, rstd, dh, tg):
    gain = scale[...].astype(F32)
    backs = slot_lanes(back[...].astype(F32), (0, 1, 2)).astype(BF)
    for c in range(4):
        cols = slice(256 * c, 256 * c + 256)
        total = dot_nt(backs, acat[cols, :])
        for w, d in zip(weights[:3], (dq, dk, dv)):
            total = total + dot_nt(d[...], w[cols, :])
        dh[:, cols] = total.astype(BF)

    def body(i, carry):
        rows = pl.ds(pl.multiple_of(i * 32, 32), 32)
        inverse = rstd[rows, :]
        xhat = (w_tok[rows, :].astype(F32) - mean[rows, :]) * inverse
        g = dh[rows, :].astype(F32) * gain
        first = jnp.mean(g, axis=-1, keepdims=True)
        second = jnp.mean(g * xhat, axis=-1, keepdims=True)
        tg[rows, :] = (w_cot[rows, :].astype(F32) + inverse * (g - first - xhat * second)).astype(BF)
        return carry

    lax.fori_loop(0, TOK // 32, body, 0)


def compute(
    sizes, w_tok, w_cot, scale, wq, wk, wv, wo, down, up, table, tg, tg_tail, gt,
    hs, q, k, v, da, at, dq, dk, dv, acat, low, back, mean, rstd, bias, dh,
):
    weights = (wq, wk, wv, wo)
    make_bias(sizes, bias)
    adapter_tables(down, acat)
    norm_rows(w_tok, scale, hs, mean, rstd)
    project(hs, w_cot, weights, up, acat, low, back, q, k, v, da)
    attend(q, k, v, da, bias, at, dq, dk, dv)
    lora_partials(hs, w_cot, at, dq, dk, dv, up, acat, low, back, gt)
    input_gradient(w_tok, w_cot, scale, weights, dq, dk, dv, acat, back, mean, rstd, dh, tg)
    for w in range(2):
        tg_tail[w] = window_to_tails(table, tg[WIN * w + 128 : WIN * w + 144, :])


def out_copies(sizes, tg, tg_tail, main, tail, send, recv):
    copies = []
    for w, p in moving_pieces():
        lat_step, lon_step = steps_of(w, p)
        device = neighbour(sizes, -lat_step, -lon_step)
        copies.append(
            remote(
                tg.at[pl.ds(WIN * w + 32 * p, 32)], main.at[w, p],
                send.at[w, p, 0], recv.at[w, p, 0], device,
            )
        )
        copies.append(
            remote(
                tg_tail.at[w, p], tail.at[w, p], send.at[w, p, 1], recv.at[w, p, 1], device
            )
        )
    return copies


class Reducer:
    def __init__(self):
        lon = lax.axis_index("lon")
        lat = lax.axis_index("lat")
        self.y = lax.rem(lon, 4)
        self.zx = lon // 4
        self.core = lax.rem(lat, 2)
        self.xl = lat // 2
        self.first = (lon, self.xl * 2 + 1 - self.core)
        self.second = []
        for n in range(1, 8):
            y = lax.rem(self.y + n // 2, 4)
            xl = lax.rem(self.xl + n % 2, 2)
            self.second.append((n - 1, y, xl, (self.zx * 4 + y, xl * 2 + self.core)))
        self.third = []
        for n in range(1, 16):
            zx = lax.rem(self.zx + n, 16)
            self.third.append((n - 1, zx, (zx * 4 + self.y, lat)))

    def partners(self):
        return [self.first] + [s[-1] for s in self.second] + [s[-1] for s in self.third]

    def start_first(self, gt, r1, sems):
        copy = remote(gt.at[1 - self.core], r1, sems.at[0, 0], sems.at[1, 0], self.first)
        copy.start()
        return copy

    def start_second(self, copy, gt, r1, s1, r2, sems):
        copy.wait()
        s1[...] = (gt[self.core].astype(F32) + r1[...].astype(F32)).astype(BF)
        copies = []
        for n, y, xl, device in self.second:
            copies.append(remote(s1.at[xl, y], r2.at[n], sems.at[0, 1 + n], sems.at[1, 1 + n], device))
            copies[-1].start()
        return copies

    def start_third(self, copies, s1, r2, s2, r3, sems):
        total = s1[self.xl, self.y].astype(F32)
        for copy in copies:
            copy.wait()
        for n in range(7):
            total = total + r2[n].astype(F32)
        for half in range(2):
            s2[half] = total[:, :, 128 * half : 128 * half + 128].astype(BF)
        copies = []
        for n, zx, device in self.third:
            copies.append(
                remote(
                    s2.at[zx // 8, lax.rem(zx, 4)], r3.at[n], sems.at[0, 8 + n], sems.at[1, 8 + n], device
                )
            )
            copies[-1].start()
        return copies

    def finish(self, copies, s2, r3, down_out, up_out, factor):
        total = s2[self.zx // 8, lax.rem(self.zx, 4)].astype(F32)
        for copy in copies:
            copy.wait()
        for n in range(15):
            total = total + r3[n].astype(F32)
        total = total * factor
        own = jnp.where(lax.rem(self.zx // 4, 2) == 0, total[:, 0:64], total[:, 64:128])
        down_out[...] = own[:, 0:32]
        up_out[...] = own[:, 32:64].T


REDUCE_SCRATCH = [
    pltpu.VMEM((2, 4, 4, 16, 256), BF),
    pltpu.VMEM((2, 4, 4, 16, 256), BF),
    pltpu.VMEM((7, 4, 16, 256), BF),
    pltpu.VMEM((2, 4, 16, 128), BF),
    pltpu.VMEM((15, 16, 128), BF),
    pltpu.SemaphoreType.DMA((2, 23)),
]


def finish_kernel(
    sizes, factor, tg, tg_tail, gt, table, grad_out, down_out, up_out,
    main, tail, send, recv, r1, s1, r2, s2, r3, sems,
):
    reducer = Reducer()
    barrier_with(ring_of(sizes) + reducer.partners())
    first = reducer.start_first(gt, r1, sems)
    copies = out_copies(sizes, tg, tg_tail, main, tail, send, recv)
    for copy in copies:
        copy.start()
    second = reducer.start_second(first, gt, r1, s1, r2, sems)
    for w in range(2):
        p = OWN[w]
        main[w, p] = tg[WIN * w + 32 * p : WIN * w + 32 * p + 32, :]
        tail[w, p] = tg_tail[w, p]
    third = reducer.start_third(second, s1, r2, s2, r3, sems)
    for copy in copies:
        copy.wait()
    unpack(table, main, tail, grad_out)
    reducer.finish(third, s2, r3, down_out, up_out, factor)


def vmem(n):
    return [pl.BlockSpec(memory_space=pltpu.VMEM)] * n


def local(
    sizes, tokens, cotangent, norm_scale_vector, query_matrix, key_matrix, value_matrix, output_matrix,
    adapter_down_maps, adapter_up_maps,
):
    table = jnp.asarray(permutation_table(), BF)
    factor = float(TOK * sizes["lon"] * sizes["lat"]) ** (-0.5)
    rows = jax.ShapeDtypeStruct((TOK, D), BF)
    w_tok, w_cot = pl.pallas_call(
        functools.partial(exchange_in, sizes),
        out_shape=(rows, rows),
        in_specs=vmem(3),
        out_specs=tuple(vmem(2)),
        scratch_shapes=[
            pltpu.VMEM((2, 2, 96, D), BF),
            pltpu.VMEM((2, 2, 4, 32, D), BF),
            pltpu.VMEM((2, 2, 4, 16, 256), BF),
            pltpu.VMEM((2, 2, 4, 16, 256), BF),
            pltpu.SemaphoreType.DMA((2, 2, 4, 2)),
            pltpu.SemaphoreType.DMA((2, 2, 4, 2)),
        ],
        compiler_params=pltpu.CompilerParams(
            collective_id=0, has_side_effects=True, vmem_limit_bytes=VMEM_LIMIT
        ),
    )(tokens, cotangent, table)
    tg, tg_tail, gt = pl.pallas_call(
        functools.partial(compute, sizes),
        out_shape=(
            rows,
            jax.ShapeDtypeStruct((2, 4, 16, 256), BF),
            jax.ShapeDtypeStruct((2, 2, 4, 4, 16, 256), BF),
        ),
        in_specs=vmem(10),
        out_specs=tuple(vmem(3)),
        scratch_shapes=[pltpu.VMEM((TOK, D), BF)] * 9
        + [
            pltpu.VMEM((D, 128), BF),
            pltpu.VMEM((TOK, 128), BF),
            pltpu.VMEM((TOK, 128), BF),
            pltpu.VMEM((TOK, 1), F32),
            pltpu.VMEM((TOK, 1), F32),
            pltpu.VMEM((2, WIN, 4 * WIN), F32),
            pltpu.VMEM((TOK, D), BF),
        ],
        compiler_params=pltpu.CompilerParams(vmem_limit_bytes=VMEM_LIMIT),
    )(
        w_tok, w_cot, norm_scale_vector.reshape(1, D), query_matrix, key_matrix, value_matrix, output_matrix,
        adapter_down_maps, adapter_up_maps, table,
    )
    return pl.pallas_call(
        functools.partial(finish_kernel, sizes, factor),
        out_shape=(
            jax.ShapeDtypeStruct(tokens.shape, BF),
            jax.ShapeDtypeStruct((16, 32), F32),
            jax.ShapeDtypeStruct((32, 16), F32),
        ),
        in_specs=vmem(4),
        out_specs=tuple(vmem(3)),
        scratch_shapes=[
            pltpu.VMEM((2, 4, 32, D), BF),
            pltpu.VMEM((2, 4, 16, 256), BF),
            pltpu.SemaphoreType.DMA((2, 4, 2)),
            pltpu.SemaphoreType.DMA((2, 4, 2)),
        ]
        + REDUCE_SCRATCH,
        compiler_params=pltpu.CompilerParams(
            collective_id=1, has_side_effects=True, vmem_limit_bytes=VMEM_LIMIT
        ),
    )(tg, tg_tail, gt, table)


def solution(mesh):
    sizes = dict(mesh.shape)
    spread = P(None, "lat", "lon", None)
    return jax.shard_map(
        functools.partial(local, sizes),
        mesh=mesh,
        in_specs=(spread, spread, P(), P(), P(), P(), P(), P(), P()),
        out_specs=(spread, P(("lon", "lat"), None), P(None, ("lon", "lat"))),
        check_vma=False,
    )
```

time: 571 us -> 80.2 us (0.14); the launches traced: 560 us -> 79.9 us
  waiting for transfers between devices: 287 us -> 0 us
  local copies, waits for them, and re-layouts: 110 us -> 12 us
  matrix products: 82 us -> 0 us
  Pallas kernels: 0 us -> 67.2 us
  other arithmetic: 40.3 us -> 0 us
  starting transfers between devices: 24.9 us -> 0 us
  between operations: 14.9 us -> 0.66 us
    psum x1 -> x0, waiting for transfers between devices: 270 us -> none  [reduce_pair(): return lax.psum((down_part, up_part), ('lon', 'lat'))]
    dot_general x34 -> x0, matrix products: 76.4 us -> none  [the longest x29 44.3 us: matrix_product(): return jnp.dot(left, right, preferred_element_type=jnp.float32)]
    pallas_call x0 -> x3, Pallas kernels: none -> 67.2 us  [the longest x1 23.6 us: local(): pl.pallas_call(functools.partial(exchange_in, sizes), out_shape=(rows, ro...]
    another operation x12 -> x0, local copies, waits for them, and re-layouts: 44.6 us -> none  [the longest x8 33.4 us: per_head(): return tensor.reshape(windows, window_extent, heads, head_size)]
    concatenate x24 -> x0, other arithmetic: 29.2 us -> none  [the longest x4 8.12 us: roll_in_four(): jnp.concatenate([arrays[projection_member][:, :, half_lon:], strips[proje...]
    slice x16 -> x0, local copies, waits for them, and re-layouts: 24.9 us -> none  [the longest x8 12.2 us: level_back(): return jnp.concatenate([region[-1:], region[:-1]], 0)]
    ppermute x16 -> x0, starting transfers between devices: 24.9 us -> none  [from_behind(): return lax.ppermute(block, axis, route)]
    reshape x10 -> x1, local copies, waits for them, and re-layouts: 19.5 us -> 1.28 us  [local(): norm_scale_vector.reshape(1, D)]
  transfers between devices with their start and end apart: 17 -> 0, of which waited for: 4 -> 0; matrix products, arithmetic and copies ran while one was open for 23% -> 0% of each run, Pallas kernels for 0% -> 0%
where the time goes in v1:
time: 80.2 us; the launch traced here: 79.9 us
  Pallas kernels  67.2 us (84%)
  local copies, waits for them, and re-layouts  12 us (15%)
    pallas_call x1, Pallas kernels, local(): pl.pallas_call(functools.partial(exchange_in, sizes), out_shape=(rows, ro...  23.6 us
    pallas_call x1, Pallas kernels, local(): pl.pallas_call(functools.partial(finish_kernel, sizes, factor), out_shape...  22.3 us
    pallas_call x1, Pallas kernels, local(): pl.pallas_call(functools.partial(compute, sizes), out_shape=(rows, jax.Sh...  21.3 us
    unnamed x6, local copies, waits for them, and re-layouts  6.97 us
    pallas_call x2, local copies, waits for them, and re-layouts, local(): pl.pallas_call(functools.partial(finish_kernel, sizes, factor), out_shape...  3.79 us

profile of v1, /device:TPU:1, one launch (start us, length us, event | category | flops | bytes accessed | tf_op | source)
XLA Modules:
  0.0 79.9 jit_solution(9475680651881988307)
XLA Ops:
  0.6 1.3 %reshape.9.scale = bf16[1,1024]{1,0:T(2,128)(2,1)} reshape(bf16[1024]{0:T(1024)(128)(2,1)} %param.12) | data formatting | bytes 4096 | tf_op jit(solution)/shard_map/reshape | solution.py:536
  1.9 0.0 copy-start
  1.9 2.2 %copy.13.tok = bf16[4,6,12,1024]{3,2,1,0:T(8,128)(2,1)} copy(bf16[4,6,12,1024]{3,0,2,1:T(4,128)(2,1)} %param.10) | data formatting | bytes 1179648 | tf_op args[0]
  4.1 2.2 %copy.14.cot = bf16[4,6,12,1024]{3,2,1,0:T(8,128)(2,1)} copy(bf16[4,6,12,1024]{3,0,2,1:T(4,128)(2,1)} %param.11) | data formatting | bytes 1179648 | tf_op args[1]
  6.3 23.6 %shard_map.121 = (bf16[288,1024]{1,0:T(8,128)(2,1)}, bf16[288,1024]{1,0:T(8,128)(2,1)}) custom-call(bf16[4,6,12,1024]{3,2,1,0:T(8,128)(2,1)} %copy.13.tok, bf16[4,6,12,1024]{3,2,1,0:T(8,128)(2,1)} %copy.14.cot, bf16[512,128]{1,0:T(8,128)(2,1)} %constant.2.clone.table), custom_call_target="tpu_custom_call" | custom-call | tf_op jit(solution)/shard_map/pallas_call | solution.py:498
  29.8 0.0 copy-done
  29.9 1.3 %copy.15.down = bf16[4,1024,32]{2,1,0:T(8,128)(2,1)} copy(bf16[4,1024,32]{1,2,0:T(8,128)(2,1)S(1)} %copy-done) | data formatting | bytes 524288 | tf_op args[7]
  31.2 21.3 %shard_map.122 = (bf16[288,1024]{1,0:T(8,128)(2,1)}, bf16[2,4,16,256]{3,2,1,0:T(8,128)(2,1)}, bf16[2,2,4,4,16,256]{5,4,3,2,1,0:T(8,128)(2,1)}) custom-call(bf16[288,1024]{1,0:T(8,128)(2,1)} %get-tuple-element.8.w_tok, bf16[288,1024]{1,0:T(8,128)(2,1)} %get-tuple-element.9.w_cot, bf16[1,1024]{1,0:T(2,128)(2,1)} %reshape.9.scale, bf16[1024,1024]{1,0:T(8,128)(2,1)} %wq.1, ...), custom_call_target="tpu_custom_call" | custom-call | tf_op jit(solution)/shard_map/pallas_call | solution.py:515
  52.5 22.3 %shard_map.123 = (bf16[4,6,12,1024]{3,2,1,0:T(8,128)(2,1)}, f32[16,32]{1,0:T(8,128)}, f32[32,16]{1,0:T(8,128)}) custom-call(bf16[288,1024]{1,0:T(8,128)(2,1)} %get-tuple-element.10.tg, bf16[2,4,16,256]{3,2,1,0:T(8,128)(2,1)} %get-tuple-element.11.tg_tail, bf16[2,2,4,4,16,256]{5,4,3,2,1,0:T(8,128)(2,1)} %get-tuple-element.12.gt, ...), custom_call_target="tpu_custom_call" | custom-call | tf_op jit(solution)/shard_map/pallas_call | solution.py:539
  74.8 2.4 %copy.16 = bf16[4,6,12,1024]{3,0,2,1:T(4,128)(2,1)} copy(bf16[4,6,12,1024]{3,2,1,0:T(8,128)(2,1)} %get-tuple-element.13) | data formatting | bytes 1179648 | tf_op jit(solution)/shard_map/pallas_call | solution.py:539
  77.2 1.4 %copy.17 = f32[32,16]{0,1:T(8,128)} copy(f32[32,16]{1,0:T(8,128)} %get-tuple-element.15) | data formatting | bytes 4096 | tf_op jit(solution)/shard_map/pallas_call | solution.py:539
  78.6 1.3 %copy.19 = f32[16,32]{1,0:T(8,128)} copy(f32[16,32]{1,0:T(8,128)} %get-tuple-element.20) | data formatting | bytes 4096
Async XLA Ops:
  1.9 27.9 %copy-start = (bf16[4,1024,32]{1,2,0:T(8,128)(2,1)S(1)}, bf16[4,1024,32]{1,2,0:T(8,128)(2,1)}, u32[]{:S(2)}) copy-start(bf16[4,1024,32]{1,2,0:T(8,128)(2,1)} %param.17) | copy-start | bytes 786436

commit v2 on v1

v2 whole, which is shorter than its diff:
```python
import functools

import jax
import jax.numpy as jnp
import numpy as np
from jax import lax
from jax.experimental import pallas as pl
from jax.experimental.pallas import tpu as pltpu
from jax.sharding import PartitionSpec as P

MESH = pl.DeviceIdType.MESH
BF = jnp.bfloat16
F32 = jnp.float32
EPS = 1e-05
NEG = -1e30
D = 1024
WIN = 144
TOK = 2 * WIN
LEVELS = ((1, 2), (3, 0))
OWN = (3, 0)
VMEM_LIMIT = 60 * 1024 * 1024


def move_tables():
    pack = np.zeros((384, 144), np.float32)
    unpack = np.zeros((288, 256), np.float32)
    ends = np.zeros((128, 64), np.float32)

    def source(w, h, t):
        return (t // 6 % 3) * 48 + (6 * h + t % 6) * 4 + LEVELS[w][t // 18]

    for w in range(2):
        for h in range(2):
            for t in range(32):
                row = 64 * w + 32 * h + t
                pack[row, source(w, h, t)] = 1
                unpack[source(w, h, t), row] = 1
            for k in range(4):
                for t in range(4):
                    row = 32 * w + 16 * h + 4 * k + t
                    pack[128 + 64 * k + row, source(w, h, 32 + t)] = 1
                    unpack[144 + source(w, h, 32 + t), 64 * k + row] = 1
    for p in range(4):
        for k in range(4):
            for t in range(4):
                ends[16 * k + 4 * p + t, 16 * p + 4 * k + t] = 1
                ends[64 + 16 * p + 4 * k + t, 16 * k + 4 * p + t] = 1
    return tuple(jnp.asarray(table, BF) for table in (pack, unpack, ends))


def dot(a, b):
    return jnp.dot(a, b, preferred_element_type=F32)


def dot_nt(a, b):
    return lax.dot_general(a, b, (((1,), (1,)), ((), ())), preferred_element_type=F32)


def dot_tn(a, b):
    return lax.dot_general(a, b, (((0,), (0,)), ((), ())), preferred_element_type=F32)


def neighbour(sizes, lat_step, lon_step):
    lon = lax.rem(lax.axis_index("lon") + lon_step + sizes["lon"], sizes["lon"])
    lat = lax.rem(lax.axis_index("lat") + lat_step + sizes["lat"], sizes["lat"])
    return (lon, lat)


def steps_of(w, p):
    differs = p ^ OWN[w]
    sign = -1 if w == 0 else 1
    return sign * (differs >> 1), sign * (differs & 1)


def moving_pieces():
    return [(w, p) for w in range(2) for p in range(4) if p != OWN[w]]


def ring_of(sizes):
    return [neighbour(sizes, *steps_of(w, p)) for w, p in moving_pieces()]


def remote(src, dst, send, recv, device):
    return pltpu.make_async_remote_copy(
        src_ref=src, dst_ref=dst, send_sem=send, recv_sem=recv, device_id=device, device_id_type=MESH
    )


def natural_rows(raw, wide):
    for a in range(6):
        for o in range(12):
            row = (12 * a + o) * 4
            wide[row : row + 4, :] = raw[a, o].astype(F32)


def piece_rows(w, p):
    return p >> 1, 64 * w + 32 * (p & 1)


def pack(wide, table, main, tail):
    for ah in range(2):
        rows = wide[WIN * ah : WIN * ah + WIN, :].astype(BF)
        main[ah] = dot(table[0:128, :], rows).astype(BF)
        ends = dot(table[128:192, :], rows[:, 0:256])
        for k in range(1, 4):
            ends = ends + dot(
                table[128 + 64 * k : 192 + 64 * k, :], rows[:, 256 * k : 256 * k + 256]
            )
        tail[ah] = ends.astype(BF)


def tails_to_window(table, tails, window, first):
    stacked = tails.reshape(64, 256)
    for k in range(4):
        window[first + 128 : first + 144, 256 * k : 256 * k + 256] = dot(
            table[16 * k : 16 * k + 16, :], stacked
        ).astype(BF)


def window_to_tails(table, rows):
    ends = jnp.zeros((64, 256), F32)
    for k in range(4):
        ends = ends + dot(
            table[64:128, 16 * k : 16 * k + 16], rows[:, 256 * k : 256 * k + 256]
        )
    return ends.astype(BF).reshape(4, 16, 256)


def in_copies(sizes, main, tail, window, tails, send, recv):
    copies = []
    for w, p in moving_pieces():
        device = neighbour(sizes, *steps_of(w, p))
        ah, row = piece_rows(w, p)
        copies.append(
            remote(
                main.at[ah, pl.ds(row, 32)], window.at[pl.ds(WIN * w + 32 * p, 32)],
                send.at[w, p, 0], recv.at[w, p, 0], device,
            )
        )
        copies.append(
            remote(
                tail.at[ah, pl.ds(row // 2, 16)], tails.at[w, p],
                send.at[w, p, 1], recv.at[w, p, 1], device,
            )
        )
    return copies


def keep_own(main, tail, window, tails):
    for w in range(2):
        p = OWN[w]
        ah, row = piece_rows(w, p)
        window[WIN * w + 32 * p : WIN * w + 32 * p + 32, :] = main[ah, row : row + 32]
        tails[w, p] = tail[ah, row // 2 : row // 2 + 16]


def out_copies(sizes, tg, tg_tail, main, tail, send, recv):
    copies = []
    for w, p in moving_pieces():
        lat_step, lon_step = steps_of(w, p)
        device = neighbour(sizes, -lat_step, -lon_step)
        ah, row = piece_rows(w, p)
        copies.append(
            remote(
                tg.at[pl.ds(WIN * w + 32 * p, 32)], main.at[ah, pl.ds(row, 32)],
                send.at[w, p, 0], recv.at[w, p, 0], device,
            )
        )
        copies.append(
            remote(
                tg_tail.at[w, p], tail.at[ah, pl.ds(row // 2, 16)],
                send.at[w, p, 1], recv.at[w, p, 1], device,
            )
        )
    return copies


def return_own(tg, tg_tail, main, tail):
    for w in range(2):
        p = OWN[w]
        ah, row = piece_rows(w, p)
        main[ah, row : row + 32] = tg[WIN * w + 32 * p : WIN * w + 32 * p + 32, :]
        tail[ah, row // 2 : row // 2 + 16] = tg_tail[w, p]


def start_barrier(devices):
    barrier = pltpu.get_barrier_semaphore()
    for device in devices:
        pl.semaphore_signal(barrier, inc=1, device_id=device, device_id_type=MESH)


def end_barrier(devices):
    pl.semaphore_wait(pltpu.get_barrier_semaphore(), len(devices))


def gain_of(scale):
    rows = scale[...].astype(F32)
    return jnp.concatenate([rows[n : n + 1] for n in range(8)], 1)


def slot_lanes(values, slots):
    lane = lax.broadcasted_iota(jnp.int32, values.shape, 1) // 32
    keep = lane == slots[0]
    for slot in slots[1:]:
        keep = keep | (lane == slot)
    return jnp.where(keep, values, 0.0)


def norm_rows(w_tok, scale, hs, mean, rstd):
    gain = gain_of(scale)

    def body(i, carry):
        rows = pl.ds(pl.multiple_of(i * 32, 32), 32)
        x = w_tok[rows, :].astype(F32)
        mu = jnp.mean(x, axis=-1, keepdims=True)
        center = x - mu
        inverse = lax.rsqrt(jnp.mean(center * center, axis=-1, keepdims=True) + EPS)
        mean[rows, :] = mu
        rstd[rows, :] = inverse
        hs[rows, :] = (center * inverse * gain).astype(BF)
        return carry

    lax.fori_loop(0, TOK // 32, body, 0)


def project_tokens(hs, weights, ups, acat, low, q, k, v):
    low[...] = dot_nt(hs[...], acat[...]).astype(BF)
    lows = [slot_lanes(low[...].astype(F32), (n,)).astype(BF) for n in range(3)]
    for c in range(4):
        cols = slice(256 * c, 256 * c + 256)
        for n, (w, out) in enumerate(zip(weights[:3], (q, k, v))):
            out[:, cols] = (dot(hs[...], w[:, cols]) + dot(lows[n], ups[:, cols])).astype(BF)


def project_cotangent(w_cot, wo, ups, acat, back, da):
    back[...] = slot_lanes(dot_nt(w_cot[...], ups[...]), (3,)).astype(BF)
    for c in range(4):
        cols = slice(256 * c, 256 * c + 256)
        da[:, cols] = (dot_nt(w_cot[...], wo[cols, :]) + dot(back[...], acat[:, cols])).astype(BF)


def make_bias(sizes, bias):
    lat = lax.axis_index("lat")

    def coordinates(r):
        tail = r >= 128
        piece = jnp.where(tail, (r - 128) // 4, r // 32)
        t = jnp.where(tail, 32 + r % 4, r % 32)
        return (piece < 2).astype(jnp.int32), (t >= 18).astype(jnp.int32)

    key_ah, key_lv = coordinates(lax.broadcasted_iota(jnp.int32, (WIN, 4 * WIN), 0))
    c = lax.broadcasted_iota(jnp.int32, (WIN, 4 * WIN), 1)
    for n in (3, 2, 1):
        c = jnp.where(c >= n * WIN, c - n * WIN, c)
    query_ah, query_lv = coordinates(c)
    for w in range(2):
        last = (lat == (sizes["lat"] - 1 if w == 0 else 0)).astype(jnp.int32)
        differs = (key_ah != query_ah).astype(jnp.int32) * last
        if w == 1:
            differs = differs + (key_lv != query_lv).astype(jnp.int32)
        bias[w] = jnp.where(differs > 0, NEG, 0.0).astype(F32)


def attend(q, k, v, da, bias, at, dq, dk, dv):
    lane = lax.broadcasted_iota(jnp.int32, (1, 256), 1) // 64
    masks = [(lane == h).astype(F32).astype(BF) for h in range(4)]
    lanes = lax.broadcasted_iota(jnp.int32, (WIN, 256), 1) // 64

    def stacked(values):
        return jnp.concatenate([values * mask for mask in masks], 0)

    def own_blocks(values):
        result = values[0:WIN]
        for h in range(1, 4):
            result = jnp.where(lanes == h, values[WIN * h : WIN * h + WIN], result)
        return result

    def body(c, carry):
        cols = pl.ds(pl.multiple_of(c * 256, 256), 256)
        for w in range(2):
            rows = pl.ds(WIN * w, WIN)
            kk = k[rows, cols]
            vv = v[rows, cols]
            q4 = stacked(q[rows, cols] * jnp.asarray(0.125, BF))
            d4 = stacked(da[rows, cols])
            s = dot_nt(kk, q4) + bias[w]
            e = jnp.exp(s - jnp.max(s, axis=0, keepdims=True))
            p = e * (1.0 / jnp.sum(e, axis=0, keepdims=True))
            dp = dot_nt(vv, d4)
            ds = (p * (dp - jnp.sum(dp * p, axis=0, keepdims=True))).astype(BF)
            pb = p.astype(BF)
            dv[rows, cols] = dot(pb, d4).astype(BF)
            dk[rows, cols] = dot(ds, q4).astype(BF)
            at[rows, cols] = own_blocks(dot_tn(pb, vv)).astype(BF)
            dq[rows, cols] = (own_blocks(dot_tn(ds, kk)) * 0.125).astype(BF)
        return carry

    lax.fori_loop(0, 4, body, 0)


def lora_partials(hs, w_cot, at, dq, dk, dv, ups, acat, low, back, gt):
    lane = lax.broadcasted_iota(jnp.int32, (TOK, 128), 1) // 32
    backs = back[...].astype(F32)
    for n, d in enumerate((dq, dk, dv)):
        backs = jnp.where(lane == n, dot_nt(d[...], ups[...]), backs)
    back[...] = backs.astype(BF)
    lows = jnp.where(lane == 3, dot_nt(at[...], acat[...]), low[...].astype(F32))
    back_t = backs.T.astype(BF)
    low_t = lows.T.astype(BF)
    for c in range(4):
        cols = slice(256 * c, 256 * c + 256)
        own_down = dot(back_t[0:96], hs[:, cols])
        last_down = dot(back_t[96:128], at[:, cols])
        ups_own = [dot(low_t[32 * n : 32 * n + 32], d[:, cols]) for n, d in enumerate((dq, dk, dv, w_cot))]
        parts = []
        for n in range(4):
            parts.append(own_down[32 * n : 32 * n + 32] if n < 3 else last_down)
            parts.append(ups_own[n])
        block = jnp.concatenate(parts, 0)
        for half in range(2):
            turned = block[:, 128 * half : 128 * half + 128].T.astype(BF)
            for b in range(8):
                f = 16 * c + 8 * half + b
                gt[f % 2, f // 2 % 2, f // 4 % 4, f // 16] = turned[16 * b : 16 * b + 16]


def hidden_gradient(chunks, weights, dq, dk, dv, acat, back, dh):
    backs = slot_lanes(back[...].astype(F32), (0, 1, 2)).astype(BF)
    for c in chunks:
        cols = slice(256 * c, 256 * c + 256)
        total = dot(backs, acat[:, cols])
        for w, d in zip(weights[:3], (dq, dk, dv)):
            total = total + dot_nt(d[...], w[cols, :])
        dh[:, cols] = total.astype(BF)


def norm_gradient(w_tok, w_cot, scale, mean, rstd, dh, tg):
    gain = gain_of(scale)

    def body(i, carry):
        rows = pl.ds(pl.multiple_of(i * 32, 32), 32)
        inverse = rstd[rows, :]
        xhat = (w_tok[rows, :].astype(F32) - mean[rows, :]) * inverse
        g = dh[rows, :].astype(F32) * gain
        first = jnp.mean(g, axis=-1, keepdims=True)
        second = jnp.mean(g * xhat, axis=-1, keepdims=True)
        tg[rows, :] = (w_cot[rows, :].astype(F32) + inverse * (g - first - xhat * second)).astype(BF)
        return carry

    lax.fori_loop(0, TOK // 32, body, 0)


class Reducer:
    def __init__(self):
        lon = lax.axis_index("lon")
        lat = lax.axis_index("lat")
        self.y = lax.rem(lon, 4)
        self.zx = lon // 4
        self.core = lax.rem(lat, 2)
        self.xl = lat // 2
        self.first = (lon, self.xl * 2 + 1 - self.core)
        self.second = []
        for n in range(1, 8):
            y = lax.rem(self.y + n // 2, 4)
            xl = lax.rem(self.xl + n % 2, 2)
            self.second.append((n - 1, y, xl, (self.zx * 4 + y, xl * 2 + self.core)))
        self.third = []
        for n in range(1, 16):
            zx = lax.rem(self.zx + n, 16)
            self.third.append((n - 1, zx, (zx * 4 + self.y, lat)))

    def partners(self):
        return [self.first] + [s[-1] for s in self.second] + [s[-1] for s in self.third]

    def start_first(self, gt, r1, sems):
        copy = remote(gt.at[1 - self.core], r1, sems.at[0, 0], sems.at[1, 0], self.first)
        copy.start()
        return copy

    def start_second(self, copy, gt, r1, s1, r2, sems):
        copy.wait()
        s1[...] = (gt[self.core].astype(F32) + r1[...].astype(F32)).astype(BF)
        copies = []
        for n, y, xl, device in self.second:
            copies.append(remote(s1.at[xl, y], r2.at[n], sems.at[0, 1 + n], sems.at[1, 1 + n], device))
            copies[-1].start()
        return copies

    def start_third(self, copies, s1, r2, s2, r3, sems):
        total = s1[self.xl, self.y].astype(F32)
        for copy in copies:
            copy.wait()
        for n in range(7):
            total = total + r2[n].astype(F32)
        for half in range(2):
            s2[half] = total[:, :, 128 * half : 128 * half + 128].astype(BF)
        copies = []
        for n, zx, device in self.third:
            copies.append(
                remote(
                    s2.at[zx // 8, lax.rem(zx, 4)], r3.at[n], sems.at[0, 8 + n], sems.at[1, 8 + n], device
                )
            )
            copies[-1].start()
        return copies

    def finish(self, copies, s2, r3, out, factor):
        total = s2[self.zx // 8, lax.rem(self.zx, 4)].astype(F32)
        for copy in copies:
            copy.wait()
        for n in range(15):
            total = total + r3[n].astype(F32)
        total = total * factor
        out[...] = jnp.where(lax.rem(self.zx // 4, 2) == 0, total[:, 0:64], total[:, 64:128])


REDUCE_SCRATCH = [
    pltpu.VMEM((2, 2, 4, 4, 16, 256), BF),
    pltpu.VMEM((2, 4, 4, 16, 256), BF),
    pltpu.VMEM((2, 4, 4, 16, 256), BF),
    pltpu.VMEM((7, 4, 16, 256), BF),
    pltpu.VMEM((2, 4, 16, 128), BF),
    pltpu.VMEM((15, 16, 128), BF),
    pltpu.SemaphoreType.DMA((2, 23)),
]
ROWS = pltpu.VMEM((TOK, D), BF)
SQUARE = pltpu.VMEM((D, D), BF)
RAW = pltpu.VMEM((6, 12, 4, D), BF)
PIECES = [pltpu.VMEM((2, 128, D), BF), pltpu.VMEM((2, 64, 256), BF), pltpu.VMEM((2, 4, 16, 256), BF)]
SEMS = pltpu.SemaphoreType.DMA((2, 4, 2))


def whole(
    sizes, factor, tok_in, cot_in, scale_in, wq_in, wk_in, wv_in, wo_in, down_in, up_in, pack_in, ends_in,
    main_out, tail_out, lora_out,
    raw_tok, raw_cot, scale, wq, wk, wv, wo, acat, ups, pack_table, ends, load, wide,
    main_tok, tail_tok, tails_tok, main_cot, tail_cot, tails_cot,
    send_tok, recv_tok, send_cot, recv_cot, send_out, recv_out,
    w_tok, w_cot, hs, q, k, v, da, at, dq, dk, dv, dh, tg, tg_tail, low, back, mean, rstd, bias,
    gt, r1, s1, r2, s2, r3, sems,
):
    reducer = Reducer()
    partners = ring_of(sizes) + reducer.partners()
    start_barrier(partners)
    moves = [
        (tok_in, raw_tok), (pack_in, pack_table), (cot_in, raw_cot), (ends_in, ends), (scale_in, scale),
        (down_in, acat), (up_in, ups), (wq_in, wq), (wk_in, wk), (wv_in, wv), (wo_in, wo),
    ]
    loads = [pltpu.make_async_copy(a, b, load.at[n]) for n, (a, b) in enumerate(moves)]
    for copy in loads:
        copy.start()
    weights = (wq, wk, wv, wo)

    loads[0].wait()
    natural_rows(raw_tok, wide)
    loads[1].wait()
    pack(wide, pack_table, main_tok, tail_tok)
    end_barrier(partners)
    tok_copies = in_copies(sizes, main_tok, tail_tok, w_tok, tails_tok, send_tok, recv_tok)
    for copy in tok_copies:
        copy.start()
    loads[2].wait()
    natural_rows(raw_cot, wide)
    pack(wide, pack_table, main_cot, tail_cot)
    cot_copies = in_copies(sizes, main_cot, tail_cot, w_cot, tails_cot, send_cot, recv_cot)
    for copy in cot_copies:
        copy.start()
    keep_own(main_tok, tail_tok, w_tok, tails_tok)
    keep_own(main_cot, tail_cot, w_cot, tails_cot)
    make_bias(sizes, bias)
    for copy in loads[3:]:
        copy.wait()
    for copy in tok_copies:
        copy.wait()
    for w in range(2):
        tails_to_window(ends, tails_tok[w], w_tok, WIN * w)
    norm_rows(w_tok, scale, hs, mean, rstd)
    project_tokens(hs, weights, ups, acat, low, q, k, v)
    for copy in cot_copies:
        copy.wait()
    for w in range(2):
        tails_to_window(ends, tails_cot[w], w_cot, WIN * w)
    project_cotangent(w_cot, wo, ups, acat, back, da)
    attend(q, k, v, da, bias, at, dq, dk, dv)
    lora_partials(hs, w_cot, at, dq, dk, dv, ups, acat, low, back, gt)
    first = reducer.start_first(gt, r1, sems)
    hidden_gradient((0, 1, 2), weights, dq, dk, dv, acat, back, dh)
    second = reducer.start_second(first, gt, r1, s1, r2, sems)
    hidden_gradient((3,), weights, dq, dk, dv, acat, back, dh)
    norm_gradient(w_tok, w_cot, scale, mean, rstd, dh, tg)
    for w in range(2):
        tg_tail[w] = window_to_tails(ends, tg[WIN * w + 128 : WIN * w + 144, :])
    out = out_copies(sizes, tg, tg_tail, main_out, tail_out, send_out, recv_out)
    for copy in out:
        copy.start()
    return_own(tg, tg_tail, main_out, tail_out)
    third = reducer.start_third(second, s1, r2, s2, r3, sems)
    for copy in out:
        copy.wait()
    reducer.finish(third, s2, r3, lora_out, factor)


def unpack(table, main, tail, lora, grad_out, down_out, up_out, wide):
    for ah in range(2):
        for k in range(4):
            cols = slice(256 * k, 256 * k + 256)
            wide[:, cols] = dot(table[0:144, 0:128], main[ah, :, cols]) + dot(
                table[144:288, 64 * k : 64 * k + 64], tail[ah]
            )
        for a in range(3):
            for o in range(12):
                row = (12 * a + o) * 4
                grad_out[3 * ah + a, o] = wide[row : row + 4, :].astype(BF)
    down_out[...] = lora[:, 0:32]
    up_out[...] = lora[:, 32:64]


def vmem(n):
    return [pl.BlockSpec(memory_space=pltpu.VMEM)] * n


def local(
    sizes, tokens, cotangent, norm_scale_vector, query_matrix, key_matrix, value_matrix, output_matrix,
    adapter_down_maps, adapter_up_maps,
):
    pack_table, unpack_table, ends = move_tables()
    factor = float(TOK * sizes["lon"] * sizes["lat"]) ** (-0.5)
    main, tail, lora = pl.pallas_call(
        functools.partial(whole, sizes, factor),
        out_shape=(
            jax.ShapeDtypeStruct((2, 128, D), BF),
            jax.ShapeDtypeStruct((2, 64, 256), BF),
            jax.ShapeDtypeStruct((16, 64), F32),
        ),
        in_specs=[pl.BlockSpec(memory_space=pl.ANY)] * 11,
        out_specs=tuple(vmem(3)),
        scratch_shapes=[
            RAW, RAW, pltpu.VMEM((8, 128), BF), SQUARE, SQUARE, SQUARE, SQUARE,
            pltpu.VMEM((128, D), BF), pltpu.VMEM((128, D), BF),
            pltpu.VMEM((384, 144), BF), pltpu.VMEM((128, 64), BF),
            pltpu.SemaphoreType.DMA((11,)), pltpu.VMEM((TOK, D), F32),
        ]
        + PIECES
        + PIECES
        + [SEMS] * 6
        + [ROWS] * 13
        + [
            pltpu.VMEM((2, 4, 16, 256), BF), pltpu.VMEM((TOK, 128), BF), pltpu.VMEM((TOK, 128), BF),
            pltpu.VMEM((TOK, 1), F32), pltpu.VMEM((TOK, 1), F32), pltpu.VMEM((2, WIN, 4 * WIN), F32),
        ]
        + REDUCE_SCRATCH,
        compiler_params=pltpu.CompilerParams(
            collective_id=0, has_side_effects=True, vmem_limit_bytes=VMEM_LIMIT
        ),
    )(
        tokens.transpose(1, 2, 0, 3), cotangent.transpose(1, 2, 0, 3), norm_scale_vector.reshape(8, 128),
        query_matrix, key_matrix, value_matrix, output_matrix,
        adapter_down_maps.transpose(0, 2, 1).reshape(128, D), adapter_up_maps.reshape(128, D), pack_table, ends,
    )
    grad, down, up = pl.pallas_call(
        unpack,
        out_shape=(
            jax.ShapeDtypeStruct((6, 12, 4, D), BF),
            jax.ShapeDtypeStruct((16, 32), F32),
            jax.ShapeDtypeStruct((16, 32), F32),
        ),
        in_specs=vmem(4),
        out_specs=tuple(vmem(3)),
        scratch_shapes=[pltpu.VMEM((WIN, D), F32)],
        compiler_params=pltpu.CompilerParams(vmem_limit_bytes=VMEM_LIMIT),
    )(unpack_table, main, tail, lora)
    return grad.transpose(2, 0, 1, 3), down, up.T


def solution(mesh):
    sizes = dict(mesh.shape)
    spread = P(None, "lat", "lon", None)
    return jax.shard_map(
        functools.partial(local, sizes),
        mesh=mesh,
        in_specs=(spread, spread, P(), P(), P(), P(), P(), P(), P()),
        out_specs=(spread, P(("lon", "lat"), None), P(None, ("lon", "lat"))),
        check_vma=False,
    )
```

time: 80.2 us -> 52.1 us (0.65)
  Pallas kernels: 67.2 us -> 51.3 us
  local copies, waits for them, and re-layouts: 12 us -> 0 us
    pallas_call x3 -> x2, Pallas kernels: 67.2 us -> 51.3 us  [the longest x1 48.9 us: local(): pl.pallas_call(functools.partial(whole, sizes, factor), out_shape=(jax.Sh...]
    unnamed x6 -> x0, local copies, waits for them, and re-layouts: 6.97 us -> none
    pallas_call x2 -> x0, local copies, waits for them, and re-layouts: 3.79 us -> none  [local(): pl.pallas_call(functools.partial(finish_kernel, sizes, factor), out_shape...]
    reshape x1 -> x0, local copies, waits for them, and re-layouts: 1.28 us -> none  [local(): norm_scale_vector.reshape(1, D)]
where the time goes in v2:
time: 52.1 us; the launch traced here: 52 us
  Pallas kernels  51.3 us (98%)
  between operations  0.64 us (1%)
    pallas_call x1, Pallas kernels, local(): pl.pallas_call(functools.partial(whole, sizes, factor), out_shape=(jax.Sh...  48.9 us
    pallas_call x1, Pallas kernels, local(): pl.pallas_call(unpack, out_shape=(jax.ShapeDtypeStruct((6, 12, 4, D), BF)...  2.44 us

profile of v2, /device:TPU:1, one launch (start us, length us, event | category | flops | bytes accessed | tf_op | source)
XLA Modules:
  0.0 52.0 jit_solution(1483524129489414237)
XLA Ops:
  0.6 48.9 %shard_map.139 = (bf16[2,128,1024]{2,1,0:T(8,128)(2,1)}, bf16[2,64,256]{2,1,0:T(8,128)(2,1)}, f32[16,64]{1,0:T(8,128)}) custom-call(bf16[6,12,4,1024]{3,2,1,0:T(4,128)(2,1)} %bitcast.9, bf16[6,12,4,1024]{3,2,1,0:T(4,128)(2,1)} %bitcast.10, bf16[8,128]{1,0:T(8,128)(2,1)} %bitcast.13, bf16[1024,1024]{1,0:T(8,128)(2,1)} %wq_in.1, bf16[1024,1024]{1,0:T(8,128)(2,1)} %wk_in.1, ...), custom_call_target="tpu_custom_call" | custom-call | tf_op jit(solution)/shard_map/pallas_call | solution.py:528
  49.5 2.4 %shard_map.140 = (bf16[6,12,4,1024]{3,2,1,0:T(4,128)(2,1)}, f32[16,32]{1,0:T(8,128)}, f32[16,32]{1,0:T(8,128)}) custom-call(bf16[288,256]{1,0:T(8,128)(2,1)} %constant.7.clone.table, bf16[2,128,1024]{2,1,0:T(8,128)(2,1)} %get-tuple-element.9.main, bf16[2,64,256]{2,1,0:T(8,128)(2,1)} %get-tuple-element.10.tail, f32[16,64]{1,0:T(8,128)} %get-tuple-element.11.lora), custom_call_target="tpu_custom_call" | custom-call | tf_op jit(solution)/shard_map/pallas_call | solution.py:560

commit v3 on v2

--- a/solution.py
+++ b/solution.py
@@ -97,9 +97,9 @@
     return p >> 1, 64 * w + 32 * (p & 1)
 
 
-def pack(wide, table, main, tail):
+def pack(natural, table, main, tail):
     for ah in range(2):
-        rows = wide[WIN * ah : WIN * ah + WIN, :].astype(BF)
+        rows = natural[WIN * ah : WIN * ah + WIN, :].astype(BF)
         main[ah] = dot(table[0:128, :], rows).astype(BF)
         ends = dot(table[128:192, :], rows[:, 0:256])
         for k in range(1, 4):
@@ -210,7 +210,7 @@
     gain = gain_of(scale)
 
     def body(i, carry):
-        rows = pl.ds(pl.multiple_of(i * 32, 32), 32)
+        rows = pl.ds(pl.multiple_of(i * 48, 48), 48)
         x = w_tok[rows, :].astype(F32)
         mu = jnp.mean(x, axis=-1, keepdims=True)
         center = x - mu
@@ -220,7 +220,7 @@
         hs[rows, :] = (center * inverse * gain).astype(BF)
         return carry
 
-    lax.fori_loop(0, TOK // 32, body, 0)
+    lax.fori_loop(0, TOK // 48, body, 0, unroll=2)
 
 
 def project_tokens(hs, weights, ups, acat, low, q, k, v):
@@ -298,16 +298,20 @@
     lax.fori_loop(0, 4, body, 0)
 
 
-def lora_partials(hs, w_cot, at, dq, dk, dv, ups, acat, low, back, gt):
+def adapter_sides(w_cot, at, dq, dk, dv, ups, acat, low, back):
     lane = lax.broadcasted_iota(jnp.int32, (TOK, 128), 1) // 32
     backs = back[...].astype(F32)
     for n, d in enumerate((dq, dk, dv)):
         backs = jnp.where(lane == n, dot_nt(d[...], ups[...]), backs)
     back[...] = backs.astype(BF)
     lows = jnp.where(lane == 3, dot_nt(at[...], acat[...]), low[...].astype(F32))
-    back_t = backs.T.astype(BF)
-    low_t = lows.T.astype(BF)
-    for c in range(4):
+    return backs.T.astype(BF), lows.T.astype(BF)
+
+
+def lora_partials(z1, sides, hs, w_cot, at, dq, dk, dv, gt):
+    back_t, low_t = sides
+    for z0 in range(2):
+        c = 2 * z1 + z0
         cols = slice(256 * c, 256 * c + 256)
         own_down = dot(back_t[0:96], hs[:, cols])
         last_down = dot(back_t[96:128], at[:, cols])
@@ -320,8 +324,10 @@
         for half in range(2):
             turned = block[:, 128 * half : 128 * half + 128].T.astype(BF)
             for b in range(8):
-                f = 16 * c + 8 * half + b
-                gt[f % 2, f // 2 % 2, f // 4 % 4, f // 16] = turned[16 * b : 16 * b + 16]
+                y, lat = 2 * half + b // 4, b % 4
+                rows = turned[16 * b : 16 * b + 16]
+                for xh in range(2):
+                    gt[lat % 2, z1, xh, lat // 2, y, z0] = rows[:, 128 * xh : 128 * xh + 128]
 
 
 def hidden_gradient(chunks, weights, dq, dk, dv, acat, back, dh):
@@ -338,7 +344,7 @@
     gain = gain_of(scale)
 
     def body(i, carry):
-        rows = pl.ds(pl.multiple_of(i * 32, 32), 32)
+        rows = pl.ds(pl.multiple_of(i * 48, 48), 48)
         inverse = rstd[rows, :]
         xhat = (w_tok[rows, :].astype(F32) - mean[rows, :]) * inverse
         g = dh[rows, :].astype(F32) * gain
@@ -347,96 +353,106 @@
         tg[rows, :] = (w_cot[rows, :].astype(F32) + inverse * (g - first - xhat * second)).astype(BF)
         return carry
 
-    lax.fori_loop(0, TOK // 32, body, 0)
+    lax.fori_loop(0, TOK // 48, body, 0, unroll=2)
 
 
 class Reducer:
     def __init__(self):
         lon = lax.axis_index("lon")
         lat = lax.axis_index("lat")
-        self.y = lax.rem(lon, 4)
-        self.zx = lon // 4
-        self.core = lax.rem(lat, 2)
-        self.xl = lat // 2
-        self.first = (lon, self.xl * 2 + 1 - self.core)
+        y = lax.rem(lon, 4)
+        z = lax.rem(lon // 4, 8)
+        xh, xl, core = lon // 32, lat // 2, lax.rem(lat, 2)
+        self.core, self.z = core, z
+        self.mine = (xh, xl, y)
+
+        def device(xh, z, y, xl, core):
+            return ((xh * 8 + z) * 4 + y, xl * 2 + core)
+
+        self.first = device(xh, z, y, xl, 1 - core)
         self.second = []
+        for n in range(1, 16):
+            to = lax.rem(xh + n // 8, 2), lax.rem(xl + n // 4, 2), lax.rem(y + n, 4)
+            self.second.append((n - 1, to, device(to[0], z, to[2], to[1], core)))
+        self.third = []
         for n in range(1, 8):
-            y = lax.rem(self.y + n // 2, 4)
-            xl = lax.rem(self.xl + n % 2, 2)
-            self.second.append((n - 1, y, xl, (self.zx * 4 + y, xl * 2 + self.core)))
-        self.third = []
-        for n in range(1, 16):
-            zx = lax.rem(self.zx + n, 16)
-            self.third.append((n - 1, zx, (zx * 4 + self.y, lat)))
+            to = lax.rem(z + n, 8)
+            self.third.append((n - 1, to, device(xh, to, y, xl, core)))
 
     def partners(self):
         return [self.first] + [s[-1] for s in self.second] + [s[-1] for s in self.third]
 
-    def start_first(self, gt, r1, sems):
-        copy = remote(gt.at[1 - self.core], r1, sems.at[0, 0], sems.at[1, 0], self.first)
+    def start_first(self, part, gt, r1, sems):
+        copy = remote(gt.at[1 - self.core, part], r1.at[part], sems.at[0, part], sems.at[1, part], self.first)
         copy.start()
         return copy
 
-    def start_second(self, copy, gt, r1, s1, r2, sems):
+    def start_second(self, part, copy, gt, r1, s1, r2, sems):
         copy.wait()
-        s1[...] = (gt[self.core].astype(F32) + r1[...].astype(F32)).astype(BF)
+        s1[part] = (gt[self.core, part].astype(F32) + r1[part].astype(F32)).astype(BF)
         copies = []
-        for n, y, xl, device in self.second:
-            copies.append(remote(s1.at[xl, y], r2.at[n], sems.at[0, 1 + n], sems.at[1, 1 + n], device))
+        for n, to, device in self.second:
+            sem = 2 + 15 * part + n
+            copies.append(
+                remote(s1.at[part, to[0], to[1], to[2]], r2.at[part, n], sems.at[0, sem], sems.at[1, sem], device)
+            )
             copies[-1].start()
         return copies
 
-    def start_third(self, copies, s1, r2, s2, r3, sems):
-        total = s1[self.xl, self.y].astype(F32)
+    def sum_second(self, part, copies, s1, r2, s2):
+        total = s1[part, self.mine[0], self.mine[1], self.mine[2]].astype(F32)
+        for copy in copies:
+            copy.wait()
+        for n in range(15):
+            total = total + r2[part, n].astype(F32)
+        s2[part] = total.astype(BF)
+
+    def start_third(self, s2, r3, sems):
+        copies = []
+        for n, to, device in self.third:
+            sem = 32 + n
+            block = s2.at[lax.rem(to // 2, 2), lax.rem(to, 2)]
+            copies.append(remote(block, r3.at[n], sems.at[0, sem], sems.at[1, sem], device))
+            copies[-1].start()
+        return copies
+
+    def finish(self, copies, s2, r3, down_out, up_out, factor):
+        total = s2[lax.rem(self.z // 2, 2), lax.rem(self.z, 2)].astype(F32)
         for copy in copies:
             copy.wait()
         for n in range(7):
-            total = total + r2[n].astype(F32)
-        for half in range(2):
-            s2[half] = total[:, :, 128 * half : 128 * half + 128].astype(BF)
-        copies = []
-        for n, zx, device in self.third:
-            copies.append(
-                remote(
-                    s2.at[zx // 8, lax.rem(zx, 4)], r3.at[n], sems.at[0, 8 + n], sems.at[1, 8 + n], device
-                )
-            )
-            copies[-1].start()
-        return copies
-
-    def finish(self, copies, s2, r3, out, factor):
-        total = s2[self.zx // 8, lax.rem(self.zx, 4)].astype(F32)
-        for copy in copies:
-            copy.wait()
-        for n in range(15):
             total = total + r3[n].astype(F32)
         total = total * factor
-        out[...] = jnp.where(lax.rem(self.zx // 4, 2) == 0, total[:, 0:64], total[:, 64:128])
+        total = jnp.where(self.z < 4, total[:, 0:64], total[:, 64:128])
+        down_out[...] = total[:, 0:32]
+        up_out[...] = total[:, 32:64]
 
 
 REDUCE_SCRATCH = [
-    pltpu.VMEM((2, 2, 4, 4, 16, 256), BF),
-    pltpu.VMEM((2, 4, 4, 16, 256), BF),
-    pltpu.VMEM((2, 4, 4, 16, 256), BF),
-    pltpu.VMEM((7, 4, 16, 256), BF),
-    pltpu.VMEM((2, 4, 16, 128), BF),
-    pltpu.VMEM((15, 16, 128), BF),
-    pltpu.SemaphoreType.DMA((2, 23)),
+    pltpu.VMEM((2, 2, 2, 2, 4, 2, 16, 128), BF),
+    pltpu.VMEM((2, 2, 2, 4, 2, 16, 128), BF),
+    pltpu.VMEM((2, 2, 2, 4, 2, 16, 128), BF),
+    pltpu.VMEM((2, 15, 2, 16, 128), BF),
+    pltpu.VMEM((2, 2, 16, 128), BF),
+    pltpu.VMEM((7, 16, 128), BF),
+    pltpu.SemaphoreType.DMA((2, 39)),
 ]
 ROWS = pltpu.VMEM((TOK, D), BF)
+WIDE = pltpu.VMEM((TOK, D), F32)
 SQUARE = pltpu.VMEM((D, D), BF)
 RAW = pltpu.VMEM((6, 12, 4, D), BF)
-PIECES = [pltpu.VMEM((2, 128, D), BF), pltpu.VMEM((2, 64, 256), BF), pltpu.VMEM((2, 4, 16, 256), BF)]
+PIECES = [pltpu.VMEM((2, 128, D), BF), pltpu.VMEM((2, 64, 256), BF)]
+TAILS = pltpu.VMEM((2, 4, 16, 256), BF)
 SEMS = pltpu.SemaphoreType.DMA((2, 4, 2))
 
 
 def whole(
     sizes, factor, tok_in, cot_in, scale_in, wq_in, wk_in, wv_in, wo_in, down_in, up_in, pack_in, ends_in,
-    main_out, tail_out, lora_out,
+    main_back, tail_back, down_out, up_out,
     raw_tok, raw_cot, scale, wq, wk, wv, wo, acat, ups, pack_table, ends, load, wide,
-    main_tok, tail_tok, tails_tok, main_cot, tail_cot, tails_cot,
+    main_tok, tail_tok, main_cot, tail_cot, tails_tok, tails_cot, tails_out,
     send_tok, recv_tok, send_cot, recv_cot, send_out, recv_out,
-    w_tok, w_cot, hs, q, k, v, da, at, dq, dk, dv, dh, tg, tg_tail, low, back, mean, rstd, bias,
+    w_tok, w_cot, hs, q, k, v, da, at, dq, dk, dv, dh, tg, low, back, mean, rstd, bias,
     gt, r1, s1, r2, s2, r3, sems,
 ):
     reducer = Reducer()
@@ -447,11 +463,13 @@
         (down_in, acat), (up_in, ups), (wq_in, wq), (wk_in, wk), (wv_in, wv), (wo_in, wo),
     ]
     loads = [pltpu.make_async_copy(a, b, load.at[n]) for n, (a, b) in enumerate(moves)]
-    for copy in loads:
+    for copy in loads[:3]:
         copy.start()
     weights = (wq, wk, wv, wo)
 
     loads[0].wait()
+    for copy in loads[3:]:
+        copy.start()
     natural_rows(raw_tok, wide)
     loads[1].wait()
     pack(wide, pack_table, main_tok, tail_tok)
@@ -459,19 +477,21 @@
     tok_copies = in_copies(sizes, main_tok, tail_tok, w_tok, tails_tok, send_tok, recv_tok)
     for copy in tok_copies:
         copy.start()
+    keep_own(main_tok, tail_tok, w_tok, tails_tok)
     loads[2].wait()
     natural_rows(raw_cot, wide)
     pack(wide, pack_table, main_cot, tail_cot)
+    keep_own(main_cot, tail_cot, w_cot, tails_cot)
+    make_bias(sizes, bias)
+    for copy in tok_copies:
+        copy.wait_send()
     cot_copies = in_copies(sizes, main_cot, tail_cot, w_cot, tails_cot, send_cot, recv_cot)
     for copy in cot_copies:
         copy.start()
-    keep_own(main_tok, tail_tok, w_tok, tails_tok)
-    keep_own(main_cot, tail_cot, w_cot, tails_cot)
-    make_bias(sizes, bias)
     for copy in loads[3:]:
         copy.wait()
     for copy in tok_copies:
-        copy.wait()
+        copy.wait_recv()
     for w in range(2):
         tails_to_window(ends, tails_tok[w], w_tok, WIN * w)
     norm_rows(w_tok, scale, hs, mean, rstd)
@@ -482,25 +502,30 @@
         tails_to_window(ends, tails_cot[w], w_cot, WIN * w)
     project_cotangent(w_cot, wo, ups, acat, back, da)
     attend(q, k, v, da, bias, at, dq, dk, dv)
-    lora_partials(hs, w_cot, at, dq, dk, dv, ups, acat, low, back, gt)
-    first = reducer.start_first(gt, r1, sems)
-    hidden_gradient((0, 1, 2), weights, dq, dk, dv, acat, back, dh)
-    second = reducer.start_second(first, gt, r1, s1, r2, sems)
-    hidden_gradient((3,), weights, dq, dk, dv, acat, back, dh)
+    sides = adapter_sides(w_cot, at, dq, dk, dv, ups, acat, low, back)
+    first = []
+    for part in range(2):
+        lora_partials(part, sides, hs, w_cot, at, dq, dk, dv, gt)
+        first.append(reducer.start_first(part, gt, r1, sems))
+    hidden_gradient((0,), weights, dq, dk, dv, acat, back, dh)
+    second = [reducer.start_second(part, first[part], gt, r1, s1, r2, sems) for part in range(2)]
+    hidden_gradient((1, 2, 3), weights, dq, dk, dv, acat, back, dh)
     norm_gradient(w_tok, w_cot, scale, mean, rstd, dh, tg)
     for w in range(2):
-        tg_tail[w] = window_to_tails(ends, tg[WIN * w + 128 : WIN * w + 144, :])
-    out = out_copies(sizes, tg, tg_tail, main_out, tail_out, send_out, recv_out)
+        tails_out[w] = window_to_tails(ends, tg[WIN * w + 128 : WIN * w + 144, :])
+    out = out_copies(sizes, tg, tails_out, main_back, tail_back, send_out, recv_out)
     for copy in out:
         copy.start()
-    return_own(tg, tg_tail, main_out, tail_out)
-    third = reducer.start_third(second, s1, r2, s2, r3, sems)
+    return_own(tg, tails_out, main_back, tail_back)
+    for part in range(2):
+        reducer.sum_second(part, second[part], s1, r2, s2)
+    third = reducer.start_third(s2, r3, sems)
     for copy in out:
         copy.wait()
-    reducer.finish(third, s2, r3, lora_out, factor)
-
-
-def unpack(table, main, tail, lora, grad_out, down_out, up_out, wide):
+    reducer.finish(third, s2, r3, down_out, up_out, factor)
+
+
+def unpack(table, main, tail, down, up, grad_out, down_out, up_out, wide):
     for ah in range(2):
         for k in range(4):
             cols = slice(256 * k, 256 * k + 256)
@@ -511,8 +536,8 @@
             for o in range(12):
                 row = (12 * a + o) * 4
                 grad_out[3 * ah + a, o] = wide[row : row + 4, :].astype(BF)
-    down_out[...] = lora[:, 0:32]
-    up_out[...] = lora[:, 32:64]
+    down_out[...] = down[...]
+    up_out[...] = up[...]
 
 
 def vmem(n):
@@ -525,27 +550,30 @@
 ):
     pack_table, unpack_table, ends = move_tables()
     factor = float(TOK * sizes["lon"] * sizes["lat"]) ** (-0.5)
-    main, tail, lora = pl.pallas_call(
+    anywhere = pl.BlockSpec(memory_space=pl.ANY)
+    results = (
+        jax.ShapeDtypeStruct((6, 12, 4, D), BF),
+        jax.ShapeDtypeStruct((16, 32), F32),
+        jax.ShapeDtypeStruct((16, 32), F32),
+    )
+    made = pl.pallas_call(
         functools.partial(whole, sizes, factor),
         out_shape=(
-            jax.ShapeDtypeStruct((2, 128, D), BF),
-            jax.ShapeDtypeStruct((2, 64, 256), BF),
-            jax.ShapeDtypeStruct((16, 64), F32),
+            jax.ShapeDtypeStruct((2, 128, D), BF), jax.ShapeDtypeStruct((2, 64, 256), BF), *results[1:],
         ),
-        in_specs=[pl.BlockSpec(memory_space=pl.ANY)] * 11,
-        out_specs=tuple(vmem(3)),
+        in_specs=[anywhere] * 11,
+        out_specs=tuple(vmem(4)),
         scratch_shapes=[
             RAW, RAW, pltpu.VMEM((8, 128), BF), SQUARE, SQUARE, SQUARE, SQUARE,
             pltpu.VMEM((128, D), BF), pltpu.VMEM((128, D), BF),
-            pltpu.VMEM((384, 144), BF), pltpu.VMEM((128, 64), BF),
-            pltpu.SemaphoreType.DMA((11,)), pltpu.VMEM((TOK, D), F32),
+            pltpu.VMEM((384, 144), BF), pltpu.VMEM((128, 64), BF), pltpu.SemaphoreType.DMA((11,)), WIDE,
         ]
-        + PIECES
-        + PIECES
+        + PIECES * 2
+        + [TAILS] * 3
         + [SEMS] * 6
         + [ROWS] * 13
         + [
-            pltpu.VMEM((2, 4, 16, 256), BF), pltpu.VMEM((TOK, 128), BF), pltpu.VMEM((TOK, 128), BF),
+            pltpu.VMEM((TOK, 128), BF), pltpu.VMEM((TOK, 128), BF),
             pltpu.VMEM((TOK, 1), F32), pltpu.VMEM((TOK, 1), F32), pltpu.VMEM((2, WIN, 4 * WIN), F32),
         ]
         + REDUCE_SCRATCH,
@@ -555,20 +583,17 @@
     )(
         tokens.transpose(1, 2, 0, 3), cotangent.transpose(1, 2, 0, 3), norm_scale_vector.reshape(8, 128),
         query_matrix, key_matrix, value_matrix, output_matrix,
-        adapter_down_maps.transpose(0, 2, 1).reshape(128, D), adapter_up_maps.reshape(128, D), pack_table, ends,
+        adapter_down_maps.transpose(0, 2, 1).reshape(128, D), adapter_up_maps.reshape(128, D),
+        pack_table, ends,
     )
     grad, down, up = pl.pallas_call(
         unpack,
-        out_shape=(
-            jax.ShapeDtypeStruct((6, 12, 4, D), BF),
-            jax.ShapeDtypeStruct((16, 32), F32),
-            jax.ShapeDtypeStruct((16, 32), F32),
-        ),
-        in_specs=vmem(4),
+        out_shape=results,
+        in_specs=vmem(5),
         out_specs=tuple(vmem(3)),
         scratch_shapes=[pltpu.VMEM((WIN, D), F32)],
         compiler_params=pltpu.CompilerParams(vmem_limit_bytes=VMEM_LIMIT),
-    )(unpack_table, main, tail, lora)
+    )(unpack_table, *made)
     return grad.transpose(2, 0, 1, 3), down, up.T
 
 

time: 52.1 us -> 50.5 us (0.969)
  Pallas kernels: 51.3 us -> 49.7 us
    pallas_call x1, Pallas kernels: 48.9 us -> 47.2 us  [local(): pl.pallas_call(functools.partial(whole, sizes, factor), out_shape=(jax.Sh...]
where the time goes in v3:
time: 50.5 us; the launch traced here: 50.3 us
  Pallas kernels  49.7 us (98%)
  between operations  0.64 us (1%)
    pallas_call x1, Pallas kernels, local(): pl.pallas_call(functools.partial(whole, sizes, factor), out_shape=(jax.Sh...  47.2 us
    pallas_call x1, Pallas kernels, local(): pl.pallas_call(unpack, out_shape=results, in_specs=vmem(5), out_specs=tup...  2.45 us

profile of v3, /device:TPU:1, one launch (start us, length us, event | category | flops | bytes accessed | tf_op | source)
XLA Modules:
  0.0 50.3 jit_solution(16002446799291423514)
XLA Ops:
  0.6 47.2 %shard_map.139 = (bf16[2,128,1024]{2,1,0:T(8,128)(2,1)}, bf16[2,64,256]{2,1,0:T(8,128)(2,1)}, f32[16,32]{1,0:T(8,128)}, f32[16,32]{1,0:T(8,128)}) custom-call(bf16[6,12,4,1024]{3,2,1,0:T(4,128)(2,1)} %bitcast.9, bf16[6,12,4,1024]{3,2,1,0:T(4,128)(2,1)} %bitcast.10, bf16[8,128]{1,0:T(8,128)(2,1)} %bitcast.13, bf16[1024,1024]{1,0:T(8,128)(2,1)} %wq_in.1, ...), custom_call_target="tpu_custom_call" | custom-call | tf_op jit(solution)/shard_map/pallas_call | solution.py:559
  47.9 2.5 %shard_map.140 = (bf16[6,12,4,1024]{3,2,1,0:T(4,128)(2,1)}, f32[16,32]{1,0:T(8,128)}, f32[16,32]{1,0:T(8,128)}) custom-call(bf16[288,256]{1,0:T(8,128)(2,1)} %constant.7.clone.table, bf16[2,128,1024]{2,1,0:T(8,128)(2,1)} %get-tuple-element.10.main, bf16[2,64,256]{2,1,0:T(8,128)(2,1)} %get-tuple-element.11.tail, f32[16,32]{1,0:T(8,128)} %get-tuple-element.12.down, ...), custom_call_target="tpu_custom_call" | custom-call | tf_op jit(solution)/shard_map/pallas_call | solution.py:589

commit v4 on v3

--- a/solution.py
+++ b/solution.py
@@ -22,8 +22,8 @@
 
 
 def move_tables():
-    pack = np.zeros((384, 144), np.float32)
-    unpack = np.zeros((288, 256), np.float32)
+    pack = np.zeros((4, 192, 144), np.float32)
+    unpack = np.zeros((4, 144, 192), np.float32)
     ends = np.zeros((128, 64), np.float32)
 
     def source(w, h, t):
@@ -33,13 +33,13 @@
         for h in range(2):
             for t in range(32):
                 row = 64 * w + 32 * h + t
-                pack[row, source(w, h, t)] = 1
-                unpack[source(w, h, t), row] = 1
+                pack[:, row, source(w, h, t)] = 1
+                unpack[:, source(w, h, t), row] = 1
             for k in range(4):
                 for t in range(4):
-                    row = 32 * w + 16 * h + 4 * k + t
-                    pack[128 + 64 * k + row, source(w, h, 32 + t)] = 1
-                    unpack[144 + source(w, h, 32 + t), 64 * k + row] = 1
+                    row = 128 + 32 * w + 16 * h + 4 * k + t
+                    pack[k, row, source(w, h, 32 + t)] = 1
+                    unpack[k, source(w, h, 32 + t), row] = 1
     for p in range(4):
         for k in range(4):
             for t in range(4):
@@ -73,7 +73,7 @@
 
 
 def moving_pieces():
-    return [(w, p) for w in range(2) for p in range(4) if p != OWN[w]]
+    return [(w, OWN[w] ^ differs) for differs in (3, 1, 2) for w in range(2)]
 
 
 def ring_of(sizes):
@@ -100,12 +100,12 @@
 def pack(natural, table, main, tail):
     for ah in range(2):
         rows = natural[WIN * ah : WIN * ah + WIN, :].astype(BF)
-        main[ah] = dot(table[0:128, :], rows).astype(BF)
-        ends = dot(table[128:192, :], rows[:, 0:256])
-        for k in range(1, 4):
-            ends = ends + dot(
-                table[128 + 64 * k : 192 + 64 * k, :], rows[:, 256 * k : 256 * k + 256]
-            )
+        ends = jnp.zeros((64, 256), F32)
+        for k in range(4):
+            cols = slice(256 * k, 256 * k + 256)
+            moved = dot(table[k], rows[:, cols])
+            main[ah, :, cols] = moved[0:128].astype(BF)
+            ends = ends + moved[128:192]
         tail[ah] = ends.astype(BF)
 
 
@@ -295,7 +295,7 @@
             dq[rows, cols] = (own_blocks(dot_tn(ds, kk)) * 0.125).astype(BF)
         return carry
 
-    lax.fori_loop(0, 4, body, 0)
+    lax.fori_loop(0, 4, body, 0, unroll=2)
 
 
 def adapter_sides(w_cot, at, dq, dk, dv, ups, acat, low, back):
@@ -457,7 +457,6 @@
 ):
     reducer = Reducer()
     partners = ring_of(sizes) + reducer.partners()
-    start_barrier(partners)
     moves = [
         (tok_in, raw_tok), (pack_in, pack_table), (cot_in, raw_cot), (ends_in, ends), (scale_in, scale),
         (down_in, acat), (up_in, ups), (wq_in, wq), (wk_in, wk), (wv_in, wv), (wo_in, wo),
@@ -465,6 +464,7 @@
     loads = [pltpu.make_async_copy(a, b, load.at[n]) for n, (a, b) in enumerate(moves)]
     for copy in loads[:3]:
         copy.start()
+    start_barrier(partners)
     weights = (wq, wk, wv, wo)
 
     loads[0].wait()
@@ -507,9 +507,11 @@
     for part in range(2):
         lora_partials(part, sides, hs, w_cot, at, dq, dk, dv, gt)
         first.append(reducer.start_first(part, gt, r1, sems))
-    hidden_gradient((0,), weights, dq, dk, dv, acat, back, dh)
-    second = [reducer.start_second(part, first[part], gt, r1, s1, r2, sems) for part in range(2)]
-    hidden_gradient((1, 2, 3), weights, dq, dk, dv, acat, back, dh)
+    second = []
+    for part in range(2):
+        hidden_gradient((part,), weights, dq, dk, dv, acat, back, dh)
+        second.append(reducer.start_second(part, first[part], gt, r1, s1, r2, sems))
+    hidden_gradient((2, 3), weights, dq, dk, dv, acat, back, dh)
     norm_gradient(w_tok, w_cot, scale, mean, rstd, dh, tg)
     for w in range(2):
         tails_out[w] = window_to_tails(ends, tg[WIN * w + 128 : WIN * w + 144, :])
@@ -529,9 +531,7 @@
     for ah in range(2):
         for k in range(4):
             cols = slice(256 * k, 256 * k + 256)
-            wide[:, cols] = dot(table[0:144, 0:128], main[ah, :, cols]) + dot(
-                table[144:288, 64 * k : 64 * k + 64], tail[ah]
-            )
+            wide[:, cols] = dot(table[k], jnp.concatenate([main[ah, :, cols], tail[ah]], 0))
         for a in range(3):
             for o in range(12):
                 row = (12 * a + o) * 4
@@ -566,7 +566,7 @@
         scratch_shapes=[
             RAW, RAW, pltpu.VMEM((8, 128), BF), SQUARE, SQUARE, SQUARE, SQUARE,
             pltpu.VMEM((128, D), BF), pltpu.VMEM((128, D), BF),
-            pltpu.VMEM((384, 144), BF), pltpu.VMEM((128, 64), BF), pltpu.SemaphoreType.DMA((11,)), WIDE,
+            pltpu.VMEM((4, 192, 144), BF), pltpu.VMEM((128, 64), BF), pltpu.SemaphoreType.DMA((11,)), WIDE,
         ]
         + PIECES * 2
         + [TAILS] * 3

time: 50.5 us -> 49.3 us (0.976)
  Pallas kernels: 49.7 us -> 48.5 us
    pallas_call x1, Pallas kernels: 47.2 us -> 46.2 us  [local(): pl.pallas_call(functools.partial(whole, sizes, factor), out_shape=(jax.Sh...]
where the time goes in v4:
time: 49.3 us; the launch traced here: 49.1 us
  Pallas kernels  48.5 us (98%)
  between operations  0.64 us (1%)
    pallas_call x1, Pallas kernels, local(): pl.pallas_call(functools.partial(whole, sizes, factor), out_shape=(jax.Sh...  46.2 us
    pallas_call x1, Pallas kernels, local(): pl.pallas_call(unpack, out_shape=results, in_specs=vmem(5), out_specs=tup...  2.35 us

profile of v4, /device:TPU:1, one launch (start us, length us, event | category | flops | bytes accessed | tf_op | source)
XLA Modules:
  0.0 49.1 jit_solution(2566805993035411884)
XLA Ops:
  0.6 46.2 %shard_map.139 = (bf16[2,128,1024]{2,1,0:T(8,128)(2,1)}, bf16[2,64,256]{2,1,0:T(8,128)(2,1)}, f32[16,32]{1,0:T(8,128)}, f32[16,32]{1,0:T(8,128)}) custom-call(bf16[6,12,4,1024]{3,2,1,0:T(4,128)(2,1)} %bitcast.9, bf16[6,12,4,1024]{3,2,1,0:T(4,128)(2,1)} %bitcast.10, bf16[8,128]{1,0:T(8,128)(2,1)} %bitcast.13, bf16[1024,1024]{1,0:T(8,128)(2,1)} %wq_in.1, ...), custom_call_target="tpu_custom_call" | custom-call | tf_op jit(solution)/shard_map/pallas_call | solution.py:559
  46.8 2.3 %shard_map.140 = (bf16[6,12,4,1024]{3,2,1,0:T(4,128)(2,1)}, f32[16,32]{1,0:T(8,128)}, f32[16,32]{1,0:T(8,128)}) custom-call(bf16[4,144,192]{2,1,0:T(8,128)(2,1)} %constant.7.clone.table, bf16[2,128,1024]{2,1,0:T(8,128)(2,1)} %get-tuple-element.10.main, bf16[2,64,256]{2,1,0:T(8,128)(2,1)} %get-tuple-element.11.tail, f32[16,32]{1,0:T(8,128)} %get-tuple-element.12.down, ...), custom_call_target="tpu_custom_call" | custom-call | tf_op jit(solution)/shard_map/pallas_call | solution.py:589

commit v5 on v4

--- a/solution.py
+++ b/solution.py
@@ -154,15 +154,17 @@
         tails[w, p] = tail[ah, row // 2 : row // 2 + 16]
 
 
-def out_copies(sizes, tg, tg_tail, main, tail, send, recv):
+def out_copies(window, sizes, tg, tg_tail, main, tail, send, recv):
     copies = []
     for w, p in moving_pieces():
+        if w != window:
+            continue
         lat_step, lon_step = steps_of(w, p)
         device = neighbour(sizes, -lat_step, -lon_step)
         ah, row = piece_rows(w, p)
         copies.append(
             remote(
-                tg.at[pl.ds(WIN * w + 32 * p, 32)], main.at[ah, pl.ds(row, 32)],
+                tg.at[pl.ds(32 * p, 32)], main.at[ah, pl.ds(row, 32)],
                 send.at[w, p, 0], recv.at[w, p, 0], device,
             )
         )
@@ -175,11 +177,11 @@
     return copies
 
 
-def return_own(tg, tg_tail, main, tail):
+def return_own(tgs, tg_tail, main, tail):
     for w in range(2):
         p = OWN[w]
         ah, row = piece_rows(w, p)
-        main[ah, row : row + 32] = tg[WIN * w + 32 * p : WIN * w + 32 * p + 32, :]
+        main[ah, row : row + 32] = tgs[w][32 * p : 32 * p + 32, :]
         tail[ah, row // 2 : row // 2 + 16] = tg_tail[w, p]
 
 
@@ -330,30 +332,27 @@
                     gt[lat % 2, z1, xh, lat // 2, y, z0] = rows[:, 128 * xh : 128 * xh + 128]
 
 
-def hidden_gradient(chunks, weights, dq, dk, dv, acat, back, dh):
-    backs = slot_lanes(back[...].astype(F32), (0, 1, 2)).astype(BF)
+def hidden_gradient(w, chunks, weights, dq, dk, dv, acat, back, dh):
+    rows = slice(WIN * w, WIN * w + WIN)
+    backs = slot_lanes(back[rows, :].astype(F32), (0, 1, 2)).astype(BF)
     for c in chunks:
         cols = slice(256 * c, 256 * c + 256)
         total = dot(backs, acat[:, cols])
-        for w, d in zip(weights[:3], (dq, dk, dv)):
-            total = total + dot_nt(d[...], w[cols, :])
-        dh[:, cols] = total.astype(BF)
-
-
-def norm_gradient(w_tok, w_cot, scale, mean, rstd, dh, tg):
+        for weight, d in zip(weights[:3], (dq, dk, dv)):
+            total = total + dot_nt(d[rows, :], weight[cols, :])
+        dh[rows, cols] = total.astype(BF)
+
+
+def norm_gradient(w, w_tok, w_cot, scale, mean, rstd, dh, tg):
     gain = gain_of(scale)
-
-    def body(i, carry):
-        rows = pl.ds(pl.multiple_of(i * 48, 48), 48)
+    for i in range(0, WIN, 48):
+        rows = slice(WIN * w + i, WIN * w + i + 48)
         inverse = rstd[rows, :]
         xhat = (w_tok[rows, :].astype(F32) - mean[rows, :]) * inverse
         g = dh[rows, :].astype(F32) * gain
         first = jnp.mean(g, axis=-1, keepdims=True)
         second = jnp.mean(g * xhat, axis=-1, keepdims=True)
-        tg[rows, :] = (w_cot[rows, :].astype(F32) + inverse * (g - first - xhat * second)).astype(BF)
-        return carry
-
-    lax.fori_loop(0, TOK // 48, body, 0, unroll=2)
+        tg[i : i + 48, :] = (w_cot[rows, :].astype(F32) + inverse * (g - first - xhat * second)).astype(BF)
 
 
 class Reducer:
@@ -371,11 +370,11 @@
 
         self.first = device(xh, z, y, xl, 1 - core)
         self.second = []
-        for n in range(1, 16):
+        for n in (10, 2, 6, 14, 9, 11, 8, 1, 3, 5, 7, 13, 15, 4, 12):
             to = lax.rem(xh + n // 8, 2), lax.rem(xl + n // 4, 2), lax.rem(y + n, 4)
             self.second.append((n - 1, to, device(to[0], z, to[2], to[1], core)))
         self.third = []
-        for n in range(1, 8):
+        for n in (4, 3, 5, 2, 6, 1, 7):
             to = lax.rem(z + n, 8)
             self.third.append((n - 1, to, device(xh, to, y, xl, core)))
 
@@ -452,7 +451,7 @@
     raw_tok, raw_cot, scale, wq, wk, wv, wo, acat, ups, pack_table, ends, load, wide,
     main_tok, tail_tok, main_cot, tail_cot, tails_tok, tails_cot, tails_out,
     send_tok, recv_tok, send_cot, recv_cot, send_out, recv_out,
-    w_tok, w_cot, hs, q, k, v, da, at, dq, dk, dv, dh, tg, low, back, mean, rstd, bias,
+    w_tok, w_cot, hs, q, k, v, da, at, dq, dk, dv, dh, tg_a, tg_b, low, back, mean, rstd, bias,
     gt, r1, s1, r2, s2, r3, sems,
 ):
     reducer = Reducer()
@@ -483,10 +482,9 @@
     pack(wide, pack_table, main_cot, tail_cot)
     keep_own(main_cot, tail_cot, w_cot, tails_cot)
     make_bias(sizes, bias)
-    for copy in tok_copies:
-        copy.wait_send()
     cot_copies = in_copies(sizes, main_cot, tail_cot, w_cot, tails_cot, send_cot, recv_cot)
-    for copy in cot_copies:
+    for ahead, copy in reversed(list(zip(tok_copies, cot_copies))):
+        ahead.wait_send()
         copy.start()
     for copy in loads[3:]:
         copy.wait()
@@ -508,17 +506,18 @@
         lora_partials(part, sides, hs, w_cot, at, dq, dk, dv, gt)
         first.append(reducer.start_first(part, gt, r1, sems))
     second = []
-    for part in range(2):
-        hidden_gradient((part,), weights, dq, dk, dv, acat, back, dh)
-        second.append(reducer.start_second(part, first[part], gt, r1, s1, r2, sems))
-    hidden_gradient((2, 3), weights, dq, dk, dv, acat, back, dh)
-    norm_gradient(w_tok, w_cot, scale, mean, rstd, dh, tg)
-    for w in range(2):
-        tails_out[w] = window_to_tails(ends, tg[WIN * w + 128 : WIN * w + 144, :])
-    out = out_copies(sizes, tg, tails_out, main_back, tail_back, send_out, recv_out)
-    for copy in out:
-        copy.start()
-    return_own(tg, tails_out, main_back, tail_back)
+    out = []
+    for w, tg in enumerate((tg_a, tg_b)):
+        for part in range(2):
+            hidden_gradient(w, (2 * part, 2 * part + 1), weights, dq, dk, dv, acat, back, dh)
+            if w == 0:
+                second.append(reducer.start_second(part, first[part], gt, r1, s1, r2, sems))
+        norm_gradient(w, w_tok, w_cot, scale, mean, rstd, dh, tg)
+        tails_out[w] = window_to_tails(ends, tg[128:144, :])
+        for copy in out_copies(w, sizes, tg, tails_out, main_back, tail_back, send_out, recv_out):
+            copy.start()
+            out.append(copy)
+    return_own((tg_a, tg_b), tails_out, main_back, tail_back)
     for part in range(2):
         reducer.sum_second(part, second[part], s1, r2, s2)
     third = reducer.start_third(s2, r3, sems)
@@ -571,7 +570,8 @@
         + PIECES * 2
         + [TAILS] * 3
         + [SEMS] * 6
-        + [ROWS] * 13
+        + [ROWS] * 12
+        + [pltpu.VMEM((WIN, D), BF)] * 2
         + [
             pltpu.VMEM((TOK, 128), BF), pltpu.VMEM((TOK, 128), BF),
             pltpu.VMEM((TOK, 1), F32), pltpu.VMEM((TOK, 1), F32), pltpu.VMEM((2, WIN, 4 * WIN), F32),

time: 49.3 us -> 48.2 us (0.978)
  Pallas kernels: 48.5 us -> 47.5 us
    pallas_call x1, Pallas kernels: 46.2 us -> 45.1 us  [local(): pl.pallas_call(functools.partial(whole, sizes, factor), out_shape=(jax.Sh...]
where the time goes in v5:
time: 48.2 us; the launch traced here: 48.1 us
  Pallas kernels  47.5 us (99%)
  between operations  0.64 us (1%)
    pallas_call x1, Pallas kernels, local(): pl.pallas_call(functools.partial(whole, sizes, factor), out_shape=(jax.Sh...  45.1 us
    pallas_call x1, Pallas kernels, local(): pl.pallas_call(unpack, out_shape=results, in_specs=vmem(5), out_specs=tup...  2.35 us

profile of v5, /device:TPU:1, one launch (start us, length us, event | category | flops | bytes accessed | tf_op | source)
XLA Modules:
  0.0 48.1 jit_solution(2715560404364650566)
XLA Ops:
  0.6 45.1 %shard_map.139 = (bf16[2,128,1024]{2,1,0:T(8,128)(2,1)}, bf16[2,64,256]{2,1,0:T(8,128)(2,1)}, f32[16,32]{1,0:T(8,128)}, f32[16,32]{1,0:T(8,128)}) custom-call(bf16[6,12,4,1024]{3,2,1,0:T(4,128)(2,1)} %bitcast.9, bf16[6,12,4,1024]{3,2,1,0:T(4,128)(2,1)} %bitcast.10, bf16[8,128]{1,0:T(8,128)(2,1)} %bitcast.13, bf16[1024,1024]{1,0:T(8,128)(2,1)} %wq_in.1, ...), custom_call_target="tpu_custom_call" | custom-call | tf_op jit(solution)/shard_map/pallas_call | solution.py:558
  45.8 2.3 %shard_map.140 = (bf16[6,12,4,1024]{3,2,1,0:T(4,128)(2,1)}, f32[16,32]{1,0:T(8,128)}, f32[16,32]{1,0:T(8,128)}) custom-call(bf16[4,144,192]{2,1,0:T(8,128)(2,1)} %constant.7.clone.table, bf16[2,128,1024]{2,1,0:T(8,128)(2,1)} %get-tuple-element.10.main, bf16[2,64,256]{2,1,0:T(8,128)(2,1)} %get-tuple-element.11.tail, f32[16,32]{1,0:T(8,128)} %get-tuple-element.12.down, ...), custom_call_target="tpu_custom_call" | custom-call | tf_op jit(solution)/shard_map/pallas_call | solution.py:589

commit v6 on v5

--- a/solution.py
+++ b/solution.py
@@ -483,7 +483,9 @@
     keep_own(main_cot, tail_cot, w_cot, tails_cot)
     make_bias(sizes, bias)
     cot_copies = in_copies(sizes, main_cot, tail_cot, w_cot, tails_cot, send_cot, recv_cot)
-    for ahead, copy in reversed(list(zip(tok_copies, cot_copies))):
+    for copy in cot_copies[:8]:
+        copy.start()
+    for ahead, copy in zip(tok_copies[8:], cot_copies[8:]):
         ahead.wait_send()
         copy.start()
     for copy in loads[3:]:
@@ -494,6 +496,8 @@
         tails_to_window(ends, tails_tok[w], w_tok, WIN * w)
     norm_rows(w_tok, scale, hs, mean, rstd)
     project_tokens(hs, weights, ups, acat, low, q, k, v)
+    for copy in tok_copies[:8]:
+        copy.wait_send()
     for copy in cot_copies:
         copy.wait()
     for w in range(2):

time: 48.2 us -> 48.7 us (1.010)
  no operation moved by 1% of the time
where the time goes in v6:
time: 48.7 us; the launch traced here: 48.6 us
  Pallas kernels  47.9 us (98%)
  between operations  0.64 us (1%)
    pallas_call x1, Pallas kernels, local(): pl.pallas_call(functools.partial(whole, sizes, factor), out_shape=(jax.Sh...  45.6 us
    pallas_call x1, Pallas kernels, local(): pl.pallas_call(unpack, out_shape=results, in_specs=vmem(5), out_specs=tup...  2.35 us

profile of v6, /device:TPU:1, one launch (start us, length us, event | category | flops | bytes accessed | tf_op | source)
XLA Modules:
  0.0 48.6 jit_solution(7051299839308460822)
XLA Ops:
  0.6 45.6 %shard_map.139 = (bf16[2,128,1024]{2,1,0:T(8,128)(2,1)}, bf16[2,64,256]{2,1,0:T(8,128)(2,1)}, f32[16,32]{1,0:T(8,128)}, f32[16,32]{1,0:T(8,128)}) custom-call(bf16[6,12,4,1024]{3,2,1,0:T(4,128)(2,1)} %bitcast.9, bf16[6,12,4,1024]{3,2,1,0:T(4,128)(2,1)} %bitcast.10, bf16[8,128]{1,0:T(8,128)(2,1)} %bitcast.13, bf16[1024,1024]{1,0:T(8,128)(2,1)} %wq_in.1, ...), custom_call_target="tpu_custom_call" | custom-call | tf_op jit(solution)/shard_map/pallas_call | solution.py:562
  46.2 2.3 %shard_map.140 = (bf16[6,12,4,1024]{3,2,1,0:T(4,128)(2,1)}, f32[16,32]{1,0:T(8,128)}, f32[16,32]{1,0:T(8,128)}) custom-call(bf16[4,144,192]{2,1,0:T(8,128)(2,1)} %constant.7.clone.table, bf16[2,128,1024]{2,1,0:T(8,128)(2,1)} %get-tuple-element.10.main, bf16[2,64,256]{2,1,0:T(8,128)(2,1)} %get-tuple-element.11.tail, f32[16,32]{1,0:T(8,128)} %get-tuple-element.12.down, ...), custom_call_target="tpu_custom_call" | custom-call | tf_op jit(solution)/shard_map/pallas_call | solution.py:593
